TPU v7x, 512 devices: a whole 4x8x8 slice. The times are simulated.
512 devices in a mesh: dom: 512 (over y, x, z, core).
Axes of the slice: x: 4, y: 8, z: 8, core: 2. Of those that a mesh axis runs over, the one named last changes fastest.
Arguments:
- base_cell: int32 [2097152], P('dom'), may hold values from 0 to 63
- offset: float32 [3, 2097152], P(None, 'dom'), may hold values from 0 to 1
- velocity: float32 [3, 2097152], P(None, 'dom'), may hold values from -4 to 4
- affine: float32 [9, 2097152], P(None, 'dom'), may hold values from -3 to 3
- strain: float32 [9, 2097152], P(None, 'dom'), may hold values from -0.1 to 0.1
- plastic: float32 [2097152], P('dom'), may hold values from 0.9 to 1.1
- particle_mass: float32 [2097152], P('dom'), may hold values from 0.5 to 2
- counts: int32 [8192], P('dom'), may hold values from 8 to 256, as said below
- neighbours: int32 [8192, 27], P('dom'), may hold values from -1 to 111, as said below
- send_rows: int32 [512, 96], P('dom'), may hold values from 0 to 15
Outputs:
- final_offset: float32 [3, 2097152], P(None, 'dom')
- final_velocity: float32 [3, 2097152], P(None, 'dom')
- final_affine: float32 [9, 2097152], P(None, 'dom')
- final_deform: float32 [9, 2097152], P(None, 'dom')
- final_plastic: float32 [2097152], P('dom')
Inputs may be any that keep to these rules, and one draw needn't show every extreme that they name: `counts`: partitions differ in density by up to a factor of four; some block holds exactly 256 particles in every draw. `neighbours`: column 13 holds each block's own index among its partition's 16 blocks; every received border block is named somewhere by its partition; -1 means no neighbour.
All inputs are finite; a program needn't handle non-finite values.
Results may differ from a plain program's by a relative error of at most 0.0003.
Values sent between devices are 32-bit elements; how exact they have to be, the bound alone decides.
A program may use at most 64 MiB of HBM per device.

v0:
```python
import jax
import jax.numpy as jnp
from jax import lax
from jax.sharding import PartitionSpec as P

HOPS = 4


DT = 0.05
SHEAR = 4.0
BULK = 4.0
HARDEN = 10.0
COMPRESS = 0.025
STRETCH = 0.0075
DENSITY = 1.0
GRAVITY = 1.0
MASS_FLOOR = 0.25
SOURCE_RIM = ((5, 6), (1, 5), (0, 1))
PAD_CORE = ((0, 3), (0, 0), (3, 0))
SOURCE_CORE = ((3, 4), (0, 4), (0, 1))
PAD_RIM = ((0, 5), (1, 1), (5, 0))


def passed_along(shard, axis, by):
    length = lax.axis_size(axis)
    pairs = [(i, i + by) for i in range(length) if 0 <= i + by < length]
    return lax.ppermute(shard, axis, pairs)


def determinant(matrix):
    return (
        matrix[0] * (matrix[4] * matrix[8] - matrix[5] * matrix[7])
        - matrix[1] * (matrix[3] * matrix[8] - matrix[5] * matrix[6])
        + matrix[2] * (matrix[3] * matrix[7] - matrix[4] * matrix[6])
    )


def project(deform, plastic):
    volume = determinant(deform)
    clamped = jnp.clip(volume, 1.0 - COMPRESS, 1.0 + STRETCH)
    hardened = plastic * volume / clamped
    factor = jnp.exp(jnp.log(clamped / volume) / 3.0)
    return (deform * factor[None], hardened, clamped)


def kirchhoff(elastic, hardened, clamped):
    factor = jnp.exp(HARDEN * (1.0 - hardened))
    shear = SHEAR * factor
    bulk = BULK * factor * jnp.log(clamped)
    entries = []
    for i in range(3):
        for j in range(3):
            inner = (
                elastic[3 * i] * elastic[3 * j]
                + elastic[3 * i + 1] * elastic[3 * j + 1]
                + elastic[3 * i + 2] * elastic[3 * j + 2]
            )
            if i == j:
                entries.append(shear * (inner - 1.0) + bulk)
            else:
                entries.append(shear * inner)
    return jnp.stack(entries)


def coordinates(cells):
    return (cells // 16, cells // 4 % 4, cells % 4)


def particle_positions(cells, offset):
    corner = coordinates(cells)
    return jnp.stack([corner[i].astype(jnp.float32) + 0.5 + offset[i] for i in range(3)])


def spline(cells, offset):
    corner = coordinates(cells)
    places = jnp.arange(6, dtype=jnp.int32)
    tables = []
    for i in range(3):
        frac = 0.5 + offset[i]
        first = 0.5 * (1.5 - frac) * (1.5 - frac)
        second = 0.75 - (frac - 1.0) * (frac - 1.0)
        third = 0.5 * (frac - 0.5) * (frac - 0.5)
        shift = places[None, None, :] - corner[i][:, :, None]
        table = (
            jnp.where(shift == 0, first[:, :, None], 0.0)
            + jnp.where(shift == 1, second[:, :, None], 0.0)
            + jnp.where(shift == 2, third[:, :, None], 0.0)
        )
        tables.append(table)
    weights = (
        tables[0][:, :, :, None, None]
        * tables[1][:, :, None, :, None]
        * tables[2][:, :, None, None, :]
    )
    return weights.reshape(cells.shape + (216,))


def node_positions():
    index = jnp.arange(216, dtype=jnp.int32)
    return jnp.stack([index // 36, index // 6 % 6, index % 6]).astype(jnp.float32)


def particle_values(mass, velocity, affine, stress, positions, live):
    volume = mass / DENSITY
    impulse = [-(4.0 * DT) * volume * stress[i] + mass * affine[i] for i in range(9)]
    carried = []
    for i in range(3):
        carried.append(
            mass * velocity[i]
            - impulse[3 * i] * positions[0]
            - impulse[3 * i + 1] * positions[1]
            - impulse[3 * i + 2] * positions[2]
        )
    values = jnp.stack([mass] + carried + impulse)
    return jnp.where(live[None], values, 0.0)


def scatter_blocks(cells, offset, values, nodes):
    weights = spline(cells, offset)
    sums = jnp.einsum("cbp,bpj->bcj", values, weights, precision=lax.Precision.HIGHEST)
    moments = []
    for i in range(3):
        total = sums[:, 1 + i]
        for j in range(3):
            total = total + sums[:, 4 + 3 * i + j] * nodes[j][None]
        moments.append(total)
    return jnp.stack([sums[:, 0]] + moments, axis=1)


def gather_particles(cells, offset, padded, nodes):
    weights = spline(cells, offset)
    positions = particle_positions(cells, offset)
    columns = [padded[:, i] for i in range(3)]
    for i in range(3):
        for j in range(3):
            columns.append(padded[:, i] * nodes[j][None])
    stacked = jnp.stack(columns, axis=1)
    result = jnp.einsum("bpj,bcj->cbp", weights, stacked, precision=lax.Precision.HIGHEST)
    speeds = result[0:3]
    entries = []
    for i in range(3):
        for j in range(3):
            entries.append(4.0 * (result[3 + 3 * i + j] - speeds[i] * positions[j]))
    return jnp.concatenate([speeds, jnp.stack(entries, axis=0)], axis=0)


def assemble_core(fetch):
    total = 0.0
    for index in range(27):
        steps = (index // 9, index // 3 % 3, index % 3)
        piece = fetch(index)
        piece = piece.reshape(piece.shape[:2] + (6, 6, 6))
        piece = piece[
            :,
            :,
            SOURCE_RIM[steps[0]][0] : SOURCE_RIM[steps[0]][1],
            SOURCE_RIM[steps[1]][0] : SOURCE_RIM[steps[1]][1],
            SOURCE_RIM[steps[2]][0] : SOURCE_RIM[steps[2]][1],
        ]
        piece = jnp.pad(
            piece, ((0, 0), (0, 0), PAD_CORE[steps[0]], PAD_CORE[steps[1]], PAD_CORE[steps[2]])
        )
        total = total + piece
    return total.reshape(total.shape[:2] + (64,))


def assemble_padded(fetch):
    total = 0.0
    for index in range(27):
        steps = (index // 9, index // 3 % 3, index % 3)
        piece = fetch(index)
        piece = piece.reshape(piece.shape[:2] + (4, 4, 4))
        piece = piece[
            :,
            :,
            SOURCE_CORE[steps[0]][0] : SOURCE_CORE[steps[0]][1],
            SOURCE_CORE[steps[1]][0] : SOURCE_CORE[steps[1]][1],
            SOURCE_CORE[steps[2]][0] : SOURCE_CORE[steps[2]][1],
        ]
        piece = jnp.pad(
            piece, ((0, 0), (0, 0), PAD_RIM[steps[0]], PAD_RIM[steps[1]], PAD_RIM[steps[2]])
        )
        total = total + piece
    return total.reshape(total.shape[:2] + (216,))


def node_speeds(totals):
    weight = jnp.maximum(totals[:, 0], MASS_FLOOR)
    down = jnp.array([0.0, 0.0, DT * GRAVITY], dtype=jnp.float32)
    return totals[:, 1:4] / weight[:, None] - down[None, :, None]


def finish(state, elastic, hardened, result, live):
    offset, velocity, affine, deform, plastic = state
    new_velocity = result[0:3]
    new_affine = result[3:12]
    new_offset = offset + DT * new_velocity
    entries = []
    for i in range(3):
        for j in range(3):
            total = elastic[3 * i + j]
            for k in range(3):
                total = total + DT * new_affine[3 * i + k] * elastic[3 * k + j]
            entries.append(total)
    new_deform = jnp.stack(entries)
    keep = live[None]
    return (
        jnp.where(keep, new_offset, offset),
        jnp.where(keep, new_velocity, velocity),
        jnp.where(keep, new_affine, affine),
        jnp.where(keep, new_deform, deform),
        jnp.where(live, hardened, plastic),
    )


def select_rows(table, index, present):
    count = table.shape[0]
    picker = ((index[..., None] == jnp.arange(count, dtype=jnp.int32)) & present[..., None]).astype(
        jnp.float32
    )
    flat = table.reshape(count, -1)
    chosen = jnp.einsum("...r,rx->...x", picker, flat, precision=lax.Precision.HIGHEST)
    return chosen.reshape(index.shape + table.shape[1:])


def send_direct(stacked, ahead, behind):
    distance = stacked.shape[0] // 2
    arrived = []
    for reach in range(1, distance + 1):
        arrived.append(ahead(stacked[reach - 1], reach))
    for reach in range(1, distance + 1):
        arrived.append(behind(stacked[distance + reach - 1], reach))
    return jnp.stack(arrived)


def deliver_partials(stacked):
    ahead = lambda piece, reach: passed_along(piece, "dom", reach)
    behind = lambda piece, reach: passed_along(piece, "dom", -reach)
    arrived = send_direct(stacked, ahead, behind)
    return arrived


def deliver_speeds(stacked):
    ahead = lambda piece, reach: passed_along(piece, "dom", reach)
    behind = lambda piece, reach: passed_along(piece, "dom", -reach)
    arrived = send_direct(stacked, ahead, behind)
    return arrived


def split_groups(array, axis):
    shape = array.shape[:axis] + (array.shape[axis] // 8, 8) + array.shape[axis + 1 :]
    return jnp.moveaxis(array.reshape(shape), axis, 0)


def advance_local(state, cells, mass, live, neighbours, rows, nodes):
    offset, velocity, affine, deform, plastic = state
    blocks, capacity = cells.shape
    elastic, hardened, clamped = project(deform, plastic)
    stress = kirchhoff(elastic, hardened, clamped)
    positions = particle_positions(cells, offset)
    values = particle_values(mass, velocity, affine, stress, positions, live)
    partial_value = lax.map(
        lambda parts: scatter_blocks(parts[0], parts[1], parts[2], nodes),
        (split_groups(cells, 0), split_groups(offset, 1), split_groups(values, 1)),
    )
    partial_value = partial_value.reshape((blocks, 4, 216))
    received = rows.shape[0]
    always = jnp.ones(rows.shape, dtype=bool)
    outgoing = select_rows(partial_value, rows, always)
    arrived = deliver_partials(
        outgoing.reshape((2 * HOPS, received // (2 * HOPS)) + outgoing.shape[1:])
    )
    arrived = arrived.reshape((received,) + outgoing.shape[1:])
    table = jnp.concatenate([partial_value, arrived], axis=0)
    present = jnp.transpose(neighbours >= 0)
    links = jnp.transpose(jnp.maximum(neighbours, 0))
    picked = select_rows(table, links, present)
    totals = assemble_core(lambda index: picked[index])
    speeds = node_speeds(totals)
    leaving = select_rows(speeds, rows, always)
    arrived_speeds = deliver_speeds(leaving.reshape((2 * HOPS, received // (2 * HOPS), 3, 64)))
    speed_table = jnp.concatenate([speeds, arrived_speeds.reshape((received, 3, 64))], axis=0)
    picked_speeds = select_rows(speed_table, links, present)
    padded = assemble_padded(lambda index: picked_speeds[index])
    result = lax.map(
        lambda parts: gather_particles(parts[0], parts[1], parts[2], nodes),
        (split_groups(cells, 0), split_groups(offset, 1), split_groups(padded, 0)),
    )
    result = jnp.moveaxis(result, 0, 1).reshape((12, blocks, capacity))
    return finish(state, elastic, hardened, result, live)


def on_device(
    base_cell,
    offset,
    velocity,
    affine,
    strain,
    plastic,
    particle_mass,
    counts,
    neighbours,
    send_rows,
):
    blocks = counts.shape[0]
    capacity = base_cell.shape[0] // blocks
    cells = base_cell.reshape(blocks, capacity)
    identity = jnp.eye(3, dtype=jnp.float32).reshape(9)
    state = (
        offset.reshape(3, blocks, capacity),
        velocity.reshape(3, blocks, capacity),
        affine.reshape(9, blocks, capacity),
        strain.reshape(9, blocks, capacity) + identity[:, None, None],
        plastic.reshape(blocks, capacity),
    )
    mass = particle_mass.reshape(blocks, capacity)
    live = jnp.arange(capacity, dtype=jnp.int32)[None, :] < counts[:, None]
    rows = send_rows.reshape(-1)
    nodes = node_positions()
    for step in range(2):
        state = advance_local(state, cells, mass, live, neighbours, rows, nodes)
    total = blocks * capacity
    return (
        state[0].reshape(3, total),
        state[1].reshape(3, total),
        state[2].reshape(9, total),
        state[3].reshape(9, total),
        state[4].reshape(total),
    )


def solution(mesh):
    return jax.shard_map(
        on_device,
        mesh=mesh,
        in_specs=(
            P("dom"),
            P(None, "dom"),
            P(None, "dom"),
            P(None, "dom"),
            P(None, "dom"),
            P("dom"),
            P("dom"),
            P("dom"),
            P("dom", None),
            P("dom", None),
        ),
        out_specs=(P(None, "dom"), P(None, "dom"), P(None, "dom"), P(None, "dom"), P("dom")),
        check_vma=False,
    )
```

profile of v0, /device:TPU:32, one launch (start us, length us, event | category | flops | bytes accessed | tf_op | source)
XLA Modules:
  0.0 214.0 jit_solution(9124975859225301895)
XLA Ops:
  3.5 2.1 slice_reduce_fusion.1
  7.3 5.0 %while.60 = (s32[]{:T(128)}, f32[2,8,4,216]{3,2,1,0:T(4,128)S(1)}, f32[2,13,8,256]{3,1,2,0:T(8,128)S(1)}, s32[2,8,256]{2,1,0:T(8,128)S(1)}, f32[2,3,8,256]{3,2,1...) while((s32[]{:T(128)}, f32[2,8,4,216]{3,2,1,0:T(4,128)S(1)}, ...), condition=%wide.region_1.2_spmd, body=%wide.region_0.1_spmd.sunk | while | flops 70064768 | bytes 5324541 | solution.py:262
  14.9 4.3 %collective-permute-start.1 = (f32[12,4,216]{2,1,0:T(4,128)S(1)}, f32[12,4,216]{2,1,0:T(4,128)S(1)}, u32[]{:S(2)}, u32[]{:S(2)}) collective-permute-start(f32[12,4,216]{2,1,0:T(4,128)S(1)} %squeeze.254), channel_id=1, source_target_pairs={{0,2},{1,3},{2,4},{3,5},{4,6},{5,7},{6,8},{7,9},{8,10},{9,11},{10,... | collective-permute-start | bytes 124424 | tf_op jit(solution)/shard_map/ppermute | solution.py:27
  19.3 6.1 %collective-permute-start.2 = (f32[12,4,216]{2,1,0:T(4,128)S(1)}, f32[12,4,216]{2,1,0:T(4,128)S(1)}, u32[]{:S(2)}, u32[]{:S(2)}) collective-permute-start(f32[12,4,216]{2,1,0:T(4,128)S(1)} %squeeze.255), channel_id=1, source_target_pairs={{0,3},{1,4},{2,5},{3,6},{4,7},{5,8},{6,9},{7,10},{8,11},{9,12},{10... | collective-permute-start | bytes 124424 | tf_op jit(solution)/shard_map/ppermute | solution.py:27
  25.5 6.4 %collective-permute-start.3 = (f32[12,4,216]{2,1,0:T(4,128)S(1)}, f32[12,4,216]{2,1,0:T(4,128)S(1)}, u32[]{:S(2)}, u32[]{:S(2)}) collective-permute-start(f32[12,4,216]{2,1,0:T(4,128)S(1)} %squeeze.256), channel_id=1, source_target_pairs={{0,4},{1,5},{2,6},{3,7},{4,8},{5,9},{6,10},{7,11},{8,12},{9,13},{1... | collective-permute-start | bytes 124424 | tf_op jit(solution)/shard_map/ppermute | solution.py:27
  32.0 7.3 %collective-permute-start.4 = (f32[12,4,216]{2,1,0:T(4,128)S(1)}, f32[12,4,216]{2,1,0:T(4,128)S(1)}, u32[]{:S(2)}, u32[]{:S(2)}) collective-permute-start(f32[12,4,216]{2,1,0:T(4,128)S(1)} %squeeze.257), channel_id=1, source_target_pairs={{1,0},{2,1},{3,2},{4,3},{5,4},{6,5},{7,6},{8,7},{9,8},{10,9},{11,1... | collective-permute-start | bytes 124424 | tf_op jit(solution)/shard_map/ppermute | solution.py:27
  41.2 2.5 %collective-permute-start.5 = (f32[12,4,216]{2,1,0:T(4,128)S(1)}, f32[12,4,216]{2,1,0:T(4,128)S(1)}, u32[]{:S(2)}, u32[]{:S(2)}) collective-permute-start(f32[12,4,216]{2,1,0:T(4,128)S(1)} %squeeze.258), channel_id=1, source_target_pairs={{2,0},{3,1},{4,2},{5,3},{6,4},{7,5},{8,6},{9,7},{10,8},{11,9},{12,... | collective-permute-start | bytes 124424 | tf_op jit(solution)/shard_map/ppermute | solution.py:27
  45.7 3.2 %collective-permute-start.7 = (f32[12,4,216]{2,1,0:T(4,128)S(1)}, f32[12,4,216]{2,1,0:T(4,128)S(1)}, u32[]{:S(2)}, u32[]{:S(2)}) collective-permute-start(f32[12,4,216]{2,1,0:T(4,128)S(1)} %squeeze.260), channel_id=1, source_target_pairs={{4,0},{5,1},{6,2},{7,3},{8,4},{9,5},{10,6},{11,7},{12,8},{13,9},{1... | collective-permute-start | bytes 124424 | tf_op jit(solution)/shard_map/ppermute | solution.py:27
  49.2 3.4 %collective-permute-done.7 = f32[12,4,216]{2,1,0:T(4,128)S(1)} collective-permute-done((f32[12,4,216]{2,1,0:T(4,128)S(1)}, f32[12,4,216]{2,1,0:T(4,128)S(1)}, u32[]{:S(2)}, u32[]{:S(2)}) %collective-permute-start.7) | collective-permute-done | bytes 41504 | tf_op jit(solution)/shard_map/ppermute | solution.py:27
  65.5 3.6 %collective-permute-start.9 = (f32[12,3,64]{2,1,0:T(4,128)S(1)}, f32[12,3,64]{2,1,0:T(4,128)S(1)}, u32[]{:S(2)}, u32[]{:S(2)}) collective-permute-start(f32[12,3,64]{2,1,0:T(4,128)S(1)} %squeeze.262), channel_id=1, source_target_pairs={{0,2},{1,3},{2,4},{3,5},{4,6},{5,7},{6,8},{7,9},{8,10},{9,11},{10,... | collective-permute-start | bytes 27656 | tf_op jit(solution)/shard_map/ppermute | solution.py:27
  69.2 4.4 %collective-permute-start.10 = (f32[12,3,64]{2,1,0:T(4,128)S(1)}, f32[12,3,64]{2,1,0:T(4,128)S(1)}, u32[]{:S(2)}, u32[]{:S(2)}) collective-permute-start(f32[12,3,64]{2,1,0:T(4,128)S(1)} %squeeze.263), channel_id=1, source_target_pairs={{0,3},{1,4},{2,5},{3,6},{4,7},{5,8},{6,9},{7,10},{8,11},{9,12},{10... | collective-permute-start | bytes 27656 | tf_op jit(solution)/shard_map/ppermute | solution.py:27
  73.7 2.0 collective-permute-start.11
  75.8 8.8 %collective-permute-start.12 = (f32[12,3,64]{2,1,0:T(4,128)S(1)}, f32[12,3,64]{2,1,0:T(4,128)S(1)}, u32[]{:S(2)}, u32[]{:S(2)}) collective-permute-start(f32[12,3,64]{2,1,0:T(4,128)S(1)} %squeeze.265), channel_id=1, source_target_pairs={{1,0},{2,1},{3,2},{4,3},{5,4},{6,5},{7,6},{8,7},{9,8},{10,9},{11,1... | collective-permute-start | bytes 27656 | tf_op jit(solution)/shard_map/ppermute | solution.py:27
  84.9 3.4 %collective-permute-start.13 = (f32[12,3,64]{2,1,0:T(4,128)S(1)}, f32[12,3,64]{2,1,0:T(4,128)S(1)}, u32[]{:S(2)}, u32[]{:S(2)}) collective-permute-start(f32[12,3,64]{2,1,0:T(4,128)S(1)} %squeeze.266), channel_id=1, source_target_pairs={{2,0},{3,1},{4,2},{5,3},{6,4},{7,5},{8,6},{9,7},{10,8},{11,9},{12,... | collective-permute-start | bytes 27656 | tf_op jit(solution)/shard_map/ppermute | solution.py:27
  88.3 3.5 %collective-permute-start.14 = (f32[12,3,64]{2,1,0:T(4,128)S(1)}, f32[12,3,64]{2,1,0:T(4,128)S(1)}, u32[]{:S(2)}, u32[]{:S(2)}) collective-permute-start(f32[12,3,64]{2,1,0:T(4,128)S(1)} %squeeze.267), channel_id=1, source_target_pairs={{3,0},{4,1},{5,2},{6,3},{7,4},{8,5},{9,6},{10,7},{11,8},{12,9},{13... | collective-permute-start | bytes 27656 | tf_op jit(solution)/shard_map/ppermute | solution.py:27
  91.8 2.1 collective-permute-start.15
  94.0 4.4 %collective-permute-done.15 = f32[12,3,64]{2,1,0:T(4,128)S(1)} collective-permute-done((f32[12,3,64]{2,1,0:T(4,128)S(1)}, f32[12,3,64]{2,1,0:T(4,128)S(1)}, u32[]{:S(2)}, u32[]{:S(2)}) %collective-permute-start.15) | collective-permute-done | bytes 9248 | tf_op jit(solution)/shard_map/ppermute | solution.py:27
  103.2 4.8 %while.61 = (s32[]{:T(128)}, f32[2,12,8,256]{3,2,0,1:T(8,128)S(1)}, f32[2,8,3,216]{3,2,1,0:T(4,128)S(1)}, f32[3,216]{1,0:T(4,128)S(1)}, s32[2,8,256]{2,1,0:T(8,1...) while((s32[]{:T(128)}, f32[2,12,8,256]{3,2,0,1:T(8,128)S(1)}, ...), condition=%wide.region_3.4_spmd, body=%wide.region_2.3_spmd.sunk | while | flops 65006788 | bytes 5939485 | solution.py:285
  114.7 5.0 %while.62 = (s32[]{:T(128)}, f32[2,8,4,216]{3,2,1,0:T(4,128)S(1)}, f32[2,13,8,256]{3,1,2,0:T(8,128)S(1)}, s32[2,8,256]{2,1,0:T(8,128)S(1)}, f32[2,3,8,256]{3,2,1...) while((s32[]{:T(128)}, f32[2,8,4,216]{3,2,1,0:T(4,128)S(1)}, ...), condition=%wide.region_5.6_spmd, body=%wide.region_4.5_spmd.sunk | while | flops 70064768 | bytes 5324541 | solution.py:262
  122.4 2.2 %collective-permute-start.17 = (f32[12,4,216]{2,1,0:T(4,128)S(1)}, f32[12,4,216]{2,1,0:T(4,128)S(1)}, u32[]{:S(2)}, u32[]{:S(2)}) collective-permute-start(f32[12,4,216]{2,1,0:T(4,128)S(1)} %squeeze.270), channel_id=1, source_target_pairs={{0,2},{1,3},{2,4},{3,5},{4,6},{5,7},{6,8},{7,9},{8,10},{9,11},{10,... | collective-permute-start | bytes 124424 | tf_op jit(solution)/shard_map/ppermute | solution.py:27
  124.7 3.1 %collective-permute-start.18 = (f32[12,4,216]{2,1,0:T(4,128)S(1)}, f32[12,4,216]{2,1,0:T(4,128)S(1)}, u32[]{:S(2)}, u32[]{:S(2)}) collective-permute-start(f32[12,4,216]{2,1,0:T(4,128)S(1)} %squeeze.271), channel_id=1, source_target_pairs={{0,3},{1,4},{2,5},{3,6},{4,7},{5,8},{6,9},{7,10},{8,11},{9,12},{10... | collective-permute-start | bytes 124424 | tf_op jit(solution)/shard_map/ppermute | solution.py:27
  130.0 8.8 %collective-permute-start.20 = (f32[12,4,216]{2,1,0:T(4,128)S(1)}, f32[12,4,216]{2,1,0:T(4,128)S(1)}, u32[]{:S(2)}, u32[]{:S(2)}) collective-permute-start(f32[12,4,216]{2,1,0:T(4,128)S(1)} %squeeze.273), channel_id=1, source_target_pairs={{1,0},{2,1},{3,2},{4,3},{5,4},{6,5},{7,6},{8,7},{9,8},{10,9},{11,1... | collective-permute-start | bytes 124424 | tf_op jit(solution)/shard_map/ppermute | solution.py:27
  139.7 3.4 %collective-permute-start.21 = (f32[12,4,216]{2,1,0:T(4,128)S(1)}, f32[12,4,216]{2,1,0:T(4,128)S(1)}, u32[]{:S(2)}, u32[]{:S(2)}) collective-permute-start(f32[12,4,216]{2,1,0:T(4,128)S(1)} %squeeze.274), channel_id=1, source_target_pairs={{2,0},{3,1},{4,2},{5,3},{6,4},{7,5},{8,6},{9,7},{10,8},{11,9},{12,... | collective-permute-start | bytes 124424 | tf_op jit(solution)/shard_map/ppermute | solution.py:27
  143.1 3.5 %collective-permute-start.22 = (f32[12,4,216]{2,1,0:T(4,128)S(1)}, f32[12,4,216]{2,1,0:T(4,128)S(1)}, u32[]{:S(2)}, u32[]{:S(2)}) collective-permute-start(f32[12,4,216]{2,1,0:T(4,128)S(1)} %squeeze.275), channel_id=1, source_target_pairs={{3,0},{4,1},{5,2},{6,3},{7,4},{8,5},{9,6},{10,7},{11,8},{12,9},{13... | collective-permute-start | bytes 124424 | tf_op jit(solution)/shard_map/ppermute | solution.py:27
  146.6 5.0 %collective-permute-start.23 = (f32[12,4,216]{2,1,0:T(4,128)S(1)}, f32[12,4,216]{2,1,0:T(4,128)S(1)}, u32[]{:S(2)}, u32[]{:S(2)}) collective-permute-start(f32[12,4,216]{2,1,0:T(4,128)S(1)} %squeeze.276), channel_id=1, source_target_pairs={{4,0},{5,1},{6,2},{7,3},{8,4},{9,5},{10,6},{11,7},{12,8},{13,9},{1... | collective-permute-start | bytes 124424 | tf_op jit(solution)/shard_map/ppermute | solution.py:27
  151.8 2.3 %collective-permute-done.23 = f32[12,4,216]{2,1,0:T(4,128)S(1)} collective-permute-done((f32[12,4,216]{2,1,0:T(4,128)S(1)}, f32[12,4,216]{2,1,0:T(4,128)S(1)}, u32[]{:S(2)}, u32[]{:S(2)}) %collective-permute-start.23) | collective-permute-done | bytes 41504 | tf_op jit(solution)/shard_map/ppermute | solution.py:27
  174.1 2.9 %collective-permute-start.26 = (f32[12,3,64]{2,1,0:T(4,128)S(1)}, f32[12,3,64]{2,1,0:T(4,128)S(1)}, u32[]{:S(2)}, u32[]{:S(2)}) collective-permute-start(f32[12,3,64]{2,1,0:T(4,128)S(1)} %squeeze.279), channel_id=1, source_target_pairs={{0,3},{1,4},{2,5},{3,6},{4,7},{5,8},{6,9},{7,10},{8,11},{9,12},{10... | collective-permute-start | bytes 27656 | tf_op jit(solution)/shard_map/ppermute | solution.py:27
  179.1 8.8 %collective-permute-start.28 = (f32[12,3,64]{2,1,0:T(4,128)S(1)}, f32[12,3,64]{2,1,0:T(4,128)S(1)}, u32[]{:S(2)}, u32[]{:S(2)}) collective-permute-start(f32[12,3,64]{2,1,0:T(4,128)S(1)} %squeeze.281), channel_id=1, source_target_pairs={{1,0},{2,1},{3,2},{4,3},{5,4},{6,5},{7,6},{8,7},{9,8},{10,9},{11,1... | collective-permute-start | bytes 27656 | tf_op jit(solution)/shard_map/ppermute | solution.py:27
  188.1 3.4 %collective-permute-start.29 = (f32[12,3,64]{2,1,0:T(4,128)S(1)}, f32[12,3,64]{2,1,0:T(4,128)S(1)}, u32[]{:S(2)}, u32[]{:S(2)}) collective-permute-start(f32[12,3,64]{2,1,0:T(4,128)S(1)} %squeeze.282), channel_id=1, source_target_pairs={{2,0},{3,1},{4,2},{5,3},{6,4},{7,5},{8,6},{9,7},{10,8},{11,9},{12,... | collective-permute-start | bytes 27656 | tf_op jit(solution)/shard_map/ppermute | solution.py:27
  191.5 3.5 %collective-permute-start.30 = (f32[12,3,64]{2,1,0:T(4,128)S(1)}, f32[12,3,64]{2,1,0:T(4,128)S(1)}, u32[]{:S(2)}, u32[]{:S(2)}) collective-permute-start(f32[12,3,64]{2,1,0:T(4,128)S(1)} %squeeze.283), channel_id=1, source_target_pairs={{3,0},{4,1},{5,2},{6,3},{7,4},{8,5},{9,6},{10,7},{11,8},{12,9},{13... | collective-permute-start | bytes 27656 | tf_op jit(solution)/shard_map/ppermute | solution.py:27
  195.0 5.6 %collective-permute-start.31 = (f32[12,3,64]{2,1,0:T(4,128)S(1)}, f32[12,3,64]{2,1,0:T(4,128)S(1)}, u32[]{:S(2)}, u32[]{:S(2)}) collective-permute-start(f32[12,3,64]{2,1,0:T(4,128)S(1)} %squeeze.284), channel_id=1, source_target_pairs={{4,0},{5,1},{6,2},{7,3},{8,4},{9,5},{10,6},{11,7},{12,8},{13,9},{1... | collective-permute-start | bytes 27656 | tf_op jit(solution)/shard_map/ppermute | solution.py:27
  206.6 4.8 %while.63 = (s32[]{:T(128)}, f32[2,12,8,256]{3,2,0,1:T(8,128)S(1)}, f32[2,8,3,216]{3,2,1,0:T(4,128)S(1)}, f32[3,216]{1,0:T(4,128)S(1)}, s32[2,8,256]{2,1,0:T(8,1...) while((s32[]{:T(128)}, f32[2,12,8,256]{3,2,0,1:T(8,128)S(1)}, ...), condition=%wide.region_7.8_spmd, body=%wide.region_6.7_spmd.sunk | while | flops 65006788 | bytes 5939485 | solution.py:285
  (792 shorter events, 88.7 us)
Async XLA Ops:
  12.9 28.3 %collective-permute-start = (f32[12,4,216]{2,1,0:T(4,128)S(1)}, f32[12,4,216]{2,1,0:T(4,128)S(1)}, u32[]{:S(2)}, u32[]{:S(2)}) collective-permute-start(f32[12,4,216]{2,1,0:T(4,128)S(1)} %squeeze.253), channel_id=1, source_target_pairs={{0,1},{1,2},{2,3},{3,4},{4,5},{5,6},{6,7},{7,8},{8,9},{9,10},{10,1... | collective-permute-start | bytes 124424 | tf_op jit(solution)/shard_map/ppermute | solution.py:27
  14.9 28.8 %collective-permute-start.1 = (f32[12,4,216]{2,1,0:T(4,128)S(1)}, f32[12,4,216]{2,1,0:T(4,128)S(1)}, u32[]{:S(2)}, u32[]{:S(2)}) collective-permute-start(f32[12,4,216]{2,1,0:T(4,128)S(1)} %squeeze.254), channel_id=1, source_target_pairs={{0,2},{1,3},{2,4},{3,5},{4,6},{5,7},{6,8},{7,9},{8,10},{9,11},{10,... | collective-permute-start | bytes 124424 | tf_op jit(solution)/shard_map/ppermute | solution.py:27
  19.3 26.4 %collective-permute-start.2 = (f32[12,4,216]{2,1,0:T(4,128)S(1)}, f32[12,4,216]{2,1,0:T(4,128)S(1)}, u32[]{:S(2)}, u32[]{:S(2)}) collective-permute-start(f32[12,4,216]{2,1,0:T(4,128)S(1)} %squeeze.255), channel_id=1, source_target_pairs={{0,3},{1,4},{2,5},{3,6},{4,7},{5,8},{6,9},{7,10},{8,11},{9,12},{10... | collective-permute-start | bytes 124424 | tf_op jit(solution)/shard_map/ppermute | solution.py:27
  25.5 23.4 %collective-permute-start.3 = (f32[12,4,216]{2,1,0:T(4,128)S(1)}, f32[12,4,216]{2,1,0:T(4,128)S(1)}, u32[]{:S(2)}, u32[]{:S(2)}) collective-permute-start(f32[12,4,216]{2,1,0:T(4,128)S(1)} %squeeze.256), channel_id=1, source_target_pairs={{0,4},{1,5},{2,6},{3,7},{4,8},{5,9},{6,10},{7,11},{8,12},{9,13},{1... | collective-permute-start | bytes 124424 | tf_op jit(solution)/shard_map/ppermute | solution.py:27
  32.0 16.9 %collective-permute-start.4 = (f32[12,4,216]{2,1,0:T(4,128)S(1)}, f32[12,4,216]{2,1,0:T(4,128)S(1)}, u32[]{:S(2)}, u32[]{:S(2)}) collective-permute-start(f32[12,4,216]{2,1,0:T(4,128)S(1)} %squeeze.257), channel_id=1, source_target_pairs={{1,0},{2,1},{3,2},{4,3},{5,4},{6,5},{7,6},{8,7},{9,8},{10,9},{11,1... | collective-permute-start | bytes 124424 | tf_op jit(solution)/shard_map/ppermute | solution.py:27
  41.2 7.7 %collective-permute-start.5 = (f32[12,4,216]{2,1,0:T(4,128)S(1)}, f32[12,4,216]{2,1,0:T(4,128)S(1)}, u32[]{:S(2)}, u32[]{:S(2)}) collective-permute-start(f32[12,4,216]{2,1,0:T(4,128)S(1)} %squeeze.258), channel_id=1, source_target_pairs={{2,0},{3,1},{4,2},{5,3},{6,4},{7,5},{8,6},{9,7},{10,8},{11,9},{12,... | collective-permute-start | bytes 124424 | tf_op jit(solution)/shard_map/ppermute | solution.py:27
  43.7 5.4 %collective-permute-start.6 = (f32[12,4,216]{2,1,0:T(4,128)S(1)}, f32[12,4,216]{2,1,0:T(4,128)S(1)}, u32[]{:S(2)}, u32[]{:S(2)}) collective-permute-start(f32[12,4,216]{2,1,0:T(4,128)S(1)} %squeeze.259), channel_id=1, source_target_pairs={{3,0},{4,1},{5,2},{6,3},{7,4},{8,5},{9,6},{10,7},{11,8},{12,9},{13... | collective-permute-start | bytes 124424 | tf_op jit(solution)/shard_map/ppermute | solution.py:27
  45.7 6.9 %collective-permute-start.7 = (f32[12,4,216]{2,1,0:T(4,128)S(1)}, f32[12,4,216]{2,1,0:T(4,128)S(1)}, u32[]{:S(2)}, u32[]{:S(2)}) collective-permute-start(f32[12,4,216]{2,1,0:T(4,128)S(1)} %squeeze.260), channel_id=1, source_target_pairs={{4,0},{5,1},{6,2},{7,3},{8,4},{9,5},{10,6},{11,7},{12,8},{13,9},{1... | collective-permute-start | bytes 124424 | tf_op jit(solution)/shard_map/ppermute | solution.py:27
  62.1 22.8 %collective-permute-start.8 = (f32[12,3,64]{2,1,0:T(4,128)S(1)}, f32[12,3,64]{2,1,0:T(4,128)S(1)}, u32[]{:S(2)}, u32[]{:S(2)}) collective-permute-start(f32[12,3,64]{2,1,0:T(4,128)S(1)} %squeeze.261), channel_id=1, source_target_pairs={{0,1},{1,2},{2,3},{3,4},{4,5},{5,6},{6,7},{7,8},{8,9},{9,10},{10,1... | collective-permute-start | bytes 27656 | tf_op jit(solution)/shard_map/ppermute | solution.py:27
  65.5 22.7 %collective-permute-start.9 = (f32[12,3,64]{2,1,0:T(4,128)S(1)}, f32[12,3,64]{2,1,0:T(4,128)S(1)}, u32[]{:S(2)}, u32[]{:S(2)}) collective-permute-start(f32[12,3,64]{2,1,0:T(4,128)S(1)} %squeeze.262), channel_id=1, source_target_pairs={{0,2},{1,3},{2,4},{3,5},{4,6},{5,7},{6,8},{7,9},{8,10},{9,11},{10,... | collective-permute-start | bytes 27656 | tf_op jit(solution)/shard_map/ppermute | solution.py:27
  69.2 22.6 %collective-permute-start.10 = (f32[12,3,64]{2,1,0:T(4,128)S(1)}, f32[12,3,64]{2,1,0:T(4,128)S(1)}, u32[]{:S(2)}, u32[]{:S(2)}) collective-permute-start(f32[12,3,64]{2,1,0:T(4,128)S(1)} %squeeze.263), channel_id=1, source_target_pairs={{0,3},{1,4},{2,5},{3,6},{4,7},{5,8},{6,9},{7,10},{8,11},{9,12},{10... | collective-permute-start | bytes 27656 | tf_op jit(solution)/shard_map/ppermute | solution.py:27
  73.7 20.2 %collective-permute-start.11 = (f32[12,3,64]{2,1,0:T(4,128)S(1)}, f32[12,3,64]{2,1,0:T(4,128)S(1)}, u32[]{:S(2)}, u32[]{:S(2)}) collective-permute-start(f32[12,3,64]{2,1,0:T(4,128)S(1)} %squeeze.264), channel_id=1, source_target_pairs={{0,4},{1,5},{2,6},{3,7},{4,8},{5,9},{6,10},{7,11},{8,12},{9,13},{1... | collective-permute-start | bytes 27656 | tf_op jit(solution)/shard_map/ppermute | solution.py:27
  75.8 18.1 %collective-permute-start.12 = (f32[12,3,64]{2,1,0:T(4,128)S(1)}, f32[12,3,64]{2,1,0:T(4,128)S(1)}, u32[]{:S(2)}, u32[]{:S(2)}) collective-permute-start(f32[12,3,64]{2,1,0:T(4,128)S(1)} %squeeze.265), channel_id=1, source_target_pairs={{1,0},{2,1},{3,2},{4,3},{5,4},{6,5},{7,6},{8,7},{9,8},{10,9},{11,1... | collective-permute-start | bytes 27656 | tf_op jit(solution)/shard_map/ppermute | solution.py:27
  84.9 9.1 %collective-permute-start.13 = (f32[12,3,64]{2,1,0:T(4,128)S(1)}, f32[12,3,64]{2,1,0:T(4,128)S(1)}, u32[]{:S(2)}, u32[]{:S(2)}) collective-permute-start(f32[12,3,64]{2,1,0:T(4,128)S(1)} %squeeze.266), channel_id=1, source_target_pairs={{2,0},{3,1},{4,2},{5,3},{6,4},{7,5},{8,6},{9,7},{10,8},{11,9},{12,... | collective-permute-start | bytes 27656 | tf_op jit(solution)/shard_map/ppermute | solution.py:27
  88.3 5.7 %collective-permute-start.14 = (f32[12,3,64]{2,1,0:T(4,128)S(1)}, f32[12,3,64]{2,1,0:T(4,128)S(1)}, u32[]{:S(2)}, u32[]{:S(2)}) collective-permute-start(f32[12,3,64]{2,1,0:T(4,128)S(1)} %squeeze.267), channel_id=1, source_target_pairs={{3,0},{4,1},{5,2},{6,3},{7,4},{8,5},{9,6},{10,7},{11,8},{12,9},{13... | collective-permute-start | bytes 27656 | tf_op jit(solution)/shard_map/ppermute | solution.py:27
  91.8 6.6 %collective-permute-start.15 = (f32[12,3,64]{2,1,0:T(4,128)S(1)}, f32[12,3,64]{2,1,0:T(4,128)S(1)}, u32[]{:S(2)}, u32[]{:S(2)}) collective-permute-start(f32[12,3,64]{2,1,0:T(4,128)S(1)} %squeeze.268), channel_id=1, source_target_pairs={{4,0},{5,1},{6,2},{7,3},{8,4},{9,5},{10,6},{11,7},{12,8},{13,9},{1... | collective-permute-start | bytes 27656 | tf_op jit(solution)/shard_map/ppermute | solution.py:27
  120.4 19.3 %collective-permute-start.16 = (f32[12,4,216]{2,1,0:T(4,128)S(1)}, f32[12,4,216]{2,1,0:T(4,128)S(1)}, u32[]{:S(2)}, u32[]{:S(2)}) collective-permute-start(f32[12,4,216]{2,1,0:T(4,128)S(1)} %squeeze.269), channel_id=1, source_target_pairs={{0,1},{1,2},{2,3},{3,4},{4,5},{5,6},{6,7},{7,8},{8,9},{9,10},{10,1... | collective-permute-start | bytes 124424 | tf_op jit(solution)/shard_map/ppermute | solution.py:27
  122.4 20.7 %collective-permute-start.17 = (f32[12,4,216]{2,1,0:T(4,128)S(1)}, f32[12,4,216]{2,1,0:T(4,128)S(1)}, u32[]{:S(2)}, u32[]{:S(2)}) collective-permute-start(f32[12,4,216]{2,1,0:T(4,128)S(1)} %squeeze.270), channel_id=1, source_target_pairs={{0,2},{1,3},{2,4},{3,5},{4,6},{5,7},{6,8},{7,9},{8,10},{9,11},{10,... | collective-permute-start | bytes 124424 | tf_op jit(solution)/shard_map/ppermute | solution.py:27
  124.7 21.9 %collective-permute-start.18 = (f32[12,4,216]{2,1,0:T(4,128)S(1)}, f32[12,4,216]{2,1,0:T(4,128)S(1)}, u32[]{:S(2)}, u32[]{:S(2)}) collective-permute-start(f32[12,4,216]{2,1,0:T(4,128)S(1)} %squeeze.271), channel_id=1, source_target_pairs={{0,3},{1,4},{2,5},{3,6},{4,7},{5,8},{6,9},{7,10},{8,11},{9,12},{10... | collective-permute-start | bytes 124424 | tf_op jit(solution)/shard_map/ppermute | solution.py:27
  127.9 23.7 %collective-permute-start.19 = (f32[12,4,216]{2,1,0:T(4,128)S(1)}, f32[12,4,216]{2,1,0:T(4,128)S(1)}, u32[]{:S(2)}, u32[]{:S(2)}) collective-permute-start(f32[12,4,216]{2,1,0:T(4,128)S(1)} %squeeze.272), channel_id=1, source_target_pairs={{0,4},{1,5},{2,6},{3,7},{4,8},{5,9},{6,10},{7,11},{8,12},{9,13},{1... | collective-permute-start | bytes 124424 | tf_op jit(solution)/shard_map/ppermute | solution.py:27
  130.0 21.7 %collective-permute-start.20 = (f32[12,4,216]{2,1,0:T(4,128)S(1)}, f32[12,4,216]{2,1,0:T(4,128)S(1)}, u32[]{:S(2)}, u32[]{:S(2)}) collective-permute-start(f32[12,4,216]{2,1,0:T(4,128)S(1)} %squeeze.273), channel_id=1, source_target_pairs={{1,0},{2,1},{3,2},{4,3},{5,4},{6,5},{7,6},{8,7},{9,8},{10,9},{11,1... | collective-permute-start | bytes 124424 | tf_op jit(solution)/shard_map/ppermute | solution.py:27
  139.7 12.0 %collective-permute-start.21 = (f32[12,4,216]{2,1,0:T(4,128)S(1)}, f32[12,4,216]{2,1,0:T(4,128)S(1)}, u32[]{:S(2)}, u32[]{:S(2)}) collective-permute-start(f32[12,4,216]{2,1,0:T(4,128)S(1)} %squeeze.274), channel_id=1, source_target_pairs={{2,0},{3,1},{4,2},{5,3},{6,4},{7,5},{8,6},{9,7},{10,8},{11,9},{12,... | collective-permute-start | bytes 124424 | tf_op jit(solution)/shard_map/ppermute | solution.py:27
  143.1 8.7 %collective-permute-start.22 = (f32[12,4,216]{2,1,0:T(4,128)S(1)}, f32[12,4,216]{2,1,0:T(4,128)S(1)}, u32[]{:S(2)}, u32[]{:S(2)}) collective-permute-start(f32[12,4,216]{2,1,0:T(4,128)S(1)} %squeeze.275), channel_id=1, source_target_pairs={{3,0},{4,1},{5,2},{6,3},{7,4},{8,5},{9,6},{10,7},{11,8},{12,9},{13... | collective-permute-start | bytes 124424 | tf_op jit(solution)/shard_map/ppermute | solution.py:27
  146.6 7.5 %collective-permute-start.23 = (f32[12,4,216]{2,1,0:T(4,128)S(1)}, f32[12,4,216]{2,1,0:T(4,128)S(1)}, u32[]{:S(2)}, u32[]{:S(2)}) collective-permute-start(f32[12,4,216]{2,1,0:T(4,128)S(1)} %squeeze.276), channel_id=1, source_target_pairs={{4,0},{5,1},{6,2},{7,3},{8,4},{9,5},{10,6},{11,7},{12,8},{13,9},{1... | collective-permute-start | bytes 124424 | tf_op jit(solution)/shard_map/ppermute | solution.py:27
  168.0 20.1 %collective-permute-start.24 = (f32[12,3,64]{2,1,0:T(4,128)S(1)}, f32[12,3,64]{2,1,0:T(4,128)S(1)}, u32[]{:S(2)}, u32[]{:S(2)}) collective-permute-start(f32[12,3,64]{2,1,0:T(4,128)S(1)} %squeeze.277), channel_id=1, source_target_pairs={{0,1},{1,2},{2,3},{3,4},{4,5},{5,6},{6,7},{7,8},{8,9},{9,10},{10,1... | collective-permute-start | bytes 27656 | tf_op jit(solution)/shard_map/ppermute | solution.py:27
  172.1 19.4 %collective-permute-start.25 = (f32[12,3,64]{2,1,0:T(4,128)S(1)}, f32[12,3,64]{2,1,0:T(4,128)S(1)}, u32[]{:S(2)}, u32[]{:S(2)}) collective-permute-start(f32[12,3,64]{2,1,0:T(4,128)S(1)} %squeeze.278), channel_id=1, source_target_pairs={{0,2},{1,3},{2,4},{3,5},{4,6},{5,7},{6,8},{7,9},{8,10},{9,11},{10,... | collective-permute-start | bytes 27656 | tf_op jit(solution)/shard_map/ppermute | solution.py:27
  174.1 20.9 %collective-permute-start.26 = (f32[12,3,64]{2,1,0:T(4,128)S(1)}, f32[12,3,64]{2,1,0:T(4,128)S(1)}, u32[]{:S(2)}, u32[]{:S(2)}) collective-permute-start(f32[12,3,64]{2,1,0:T(4,128)S(1)} %squeeze.279), channel_id=1, source_target_pairs={{0,3},{1,4},{2,5},{3,6},{4,7},{5,8},{6,9},{7,10},{8,11},{9,12},{10... | collective-permute-start | bytes 27656 | tf_op jit(solution)/shard_map/ppermute | solution.py:27
  177.1 23.5 %collective-permute-start.27 = (f32[12,3,64]{2,1,0:T(4,128)S(1)}, f32[12,3,64]{2,1,0:T(4,128)S(1)}, u32[]{:S(2)}, u32[]{:S(2)}) collective-permute-start(f32[12,3,64]{2,1,0:T(4,128)S(1)} %squeeze.280), channel_id=1, source_target_pairs={{0,4},{1,5},{2,6},{3,7},{4,8},{5,9},{6,10},{7,11},{8,12},{9,13},{1... | collective-permute-start | bytes 27656 | tf_op jit(solution)/shard_map/ppermute | solution.py:27
  179.1 21.6 %collective-permute-start.28 = (f32[12,3,64]{2,1,0:T(4,128)S(1)}, f32[12,3,64]{2,1,0:T(4,128)S(1)}, u32[]{:S(2)}, u32[]{:S(2)}) collective-permute-start(f32[12,3,64]{2,1,0:T(4,128)S(1)} %squeeze.281), channel_id=1, source_target_pairs={{1,0},{2,1},{3,2},{4,3},{5,4},{6,5},{7,6},{8,7},{9,8},{10,9},{11,1... | collective-permute-start | bytes 27656 | tf_op jit(solution)/shard_map/ppermute | solution.py:27
  188.1 12.6 %collective-permute-start.29 = (f32[12,3,64]{2,1,0:T(4,128)S(1)}, f32[12,3,64]{2,1,0:T(4,128)S(1)}, u32[]{:S(2)}, u32[]{:S(2)}) collective-permute-start(f32[12,3,64]{2,1,0:T(4,128)S(1)} %squeeze.282), channel_id=1, source_target_pairs={{2,0},{3,1},{4,2},{5,3},{6,4},{7,5},{8,6},{9,7},{10,8},{11,9},{12,... | collective-permute-start | bytes 27656 | tf_op jit(solution)/shard_map/ppermute | solution.py:27
  191.5 9.2 %collective-permute-start.30 = (f32[12,3,64]{2,1,0:T(4,128)S(1)}, f32[12,3,64]{2,1,0:T(4,128)S(1)}, u32[]{:S(2)}, u32[]{:S(2)}) collective-permute-start(f32[12,3,64]{2,1,0:T(4,128)S(1)} %squeeze.283), channel_id=1, source_target_pairs={{3,0},{4,1},{5,2},{6,3},{7,4},{8,5},{9,6},{10,7},{11,8},{12,9},{13... | collective-permute-start | bytes 27656 | tf_op jit(solution)/shard_map/ppermute | solution.py:27
  195.0 6.8 %collective-permute-start.31 = (f32[12,3,64]{2,1,0:T(4,128)S(1)}, f32[12,3,64]{2,1,0:T(4,128)S(1)}, u32[]{:S(2)}, u32[]{:S(2)}) collective-permute-start(f32[12,3,64]{2,1,0:T(4,128)S(1)} %squeeze.284), channel_id=1, source_target_pairs={{4,0},{5,1},{6,2},{7,3},{8,4},{9,5},{10,6},{11,7},{12,8},{13,9},{1... | collective-permute-start | bytes 27656 | tf_op jit(solution)/shard_map/ppermute | solution.py:27
  (45 other events, 348.6 us)
where the time goes:
time: 215 us; the launch traced here: 214 us
  starting transfers between devices  123 us (57%)
  local copies, waits for them, and re-layouts  42.8 us (20%)
  matrix products  17 us (8%)
  other arithmetic  14.3 us (7%)
  waiting for transfers between devices  11.5 us (5%)
  between operations  4.39 us (2%)
    ppermute x32, starting transfers between devices, passed_along(): return lax.ppermute(shard, axis, pairs)  123 us
    ppermute x32, waiting for transfers between devices, passed_along(): return lax.ppermute(shard, axis, pairs)  11.5 us
    slice x58, local copies, waits for them, and re-layouts, advance_local(): totals = assemble_core(lambda index: picked[index])  10.3 us
    dot_general x4, matrix products, scatter_blocks(): jnp.einsum('cbp,bpj->bcj', values, weights, precision=lax.Precision.HIGHEST)  7.6 us
    unnamed x153, local copies, waits for them, and re-layouts  5.85 us
    dot_general x4, matrix products, gather_particles(): jnp.einsum('bpj,bcj->cbp', weights, stacked, precision=lax.Precision.HIGH...  5.64 us
    slice x58, local copies, waits for them, and re-layouts, advance_local(): padded = assemble_padded(lambda index: picked_speeds[index])  5.48 us
    unnamed x12, other arithmetic  4.94 us
  transfers between devices with their start and end apart: 32, of which 5 were waited for; matrix products, arithmetic and copies ran while one was open for 4% of the time, Pallas kernels for 0%

commit v1 on v0

v1 whole, which is shorter than its diff:
```python
import jax
import jax.numpy as jnp
import numpy as np
from jax import lax
from jax.experimental import pallas as pl
from jax.experimental.pallas import tpu as pltpu
from jax.sharding import PartitionSpec as P

OWN = 16
PMAX = 256
HOPS = 4
SLOTS = 12
GROUPS = 2 * HOPS
RECEIVED = GROUPS * SLOTS
NONE = OWN + RECEIVED
PARTICLES = OWN * PMAX
TILES = PARTICLES // 128

DT = 0.05
SHEAR = 4.0
BULK = 4.0
HARDEN = 10.0
COMPRESS = 0.025
STRETCH = 0.0075
GRAVITY = 1.0
MASS_FLOOR = 0.25


def tables():
    row = np.arange(8)[:, None]
    lane = np.arange(128)[None, :]
    half = row // 4 + 0 * lane
    third = lane // 36 + 0 * row
    place = lane % 36 + 0 * row
    inside = third < 3
    node = [3 * half + third, place // 6, place % 6]
    step = [(x == 0).astype(int) - (x == 5).astype(int) for x in node]
    offset_id = 9 * (step[0] + 1) + 3 * (step[1] + 1) + step[2] + 1
    offset_id = np.where(inside, offset_id, 13)
    core = [(x + 3) % 4 for x in node]
    core_id = np.where(inside, 16 * core[0] + 4 * core[1] + core[2], -1)
    fold = np.zeros((128, 128), np.float32)
    for h in range(2):
        for l in range(108):
            fold[l, 64 * h + core_id[4 * h, l]] = 1.0
    spot = np.arange(40)
    wide = np.zeros((40, 128))
    consts = np.concatenate(
        [
            wide + (spot // 6)[:, None],
            wide + (spot % 6)[:, None],
            3 * half,
            offset_id,
        ]
    ).astype(np.float32)
    gather = np.concatenate([fold, fold])
    spread = np.concatenate([fold.T, fold.T])
    return consts, gather, spread


def determinant(m):
    return (
        m[0] * (m[4] * m[8] - m[5] * m[7])
        - m[1] * (m[3] * m[8] - m[5] * m[6])
        + m[2] * (m[3] * m[7] - m[4] * m[6])
    )


def low_part(x):
    return x - x.astype(jnp.bfloat16).astype(jnp.float32)


def high_low(x, axis):
    return jnp.concatenate([x, low_part(x)], axis=axis).astype(jnp.bfloat16)


def dot_nt(a, b):
    return lax.dot_general(a, b, (((1,), (1,)), ((), ())), preferred_element_type=jnp.float32)


def dot_nn(a, b):
    return lax.dot_general(a, b, (((1,), (0,)), ((), ())), preferred_element_type=jnp.float32)


def weight(node, spots):
    cell, _, first, second, third = spots
    shift = node - cell
    value = jnp.where(shift == 2.0, third, 0.0)
    value = jnp.where(shift == 1.0, second, value)
    return jnp.where(shift == 0.0, first, value)


def pair(ref, b):
    both = ref[pl.ds(pl.multiple_of(16 * b, 16), 16), :]
    return jnp.concatenate([both[0:8], both[8:16]], axis=1)


def partner(me, group, length):
    by = group + 1 if group < HOPS else -(group - HOPS + 1)
    return lax.rem(me + (by + length), length)


def step_kernel(
    length,
    links,
    rows,
    cells,
    offset_in,
    velocity_in,
    affine_in,
    strain_in,
    plastic_in,
    mass_in,
    live_in,
    consts,
    gather_mat,
    spread_mat,
    offset_out,
    velocity_out,
    affine_out,
    deform_out,
    plastic_out,
    move,
    affine8,
    deform8,
    ninth,
    plastic,
    elastic,
    part_a,
    part_b,
    part_c,
    part_d,
    spots_a,
    spots_b,
    weight_hi,
    weight_lo,
    first_w,
    first_d,
    own,
    table,
    leaving,
    speed,
    speed_side,
    speed_out,
    speed_in,
    padded,
    field,
    found_a,
    found_b,
    send_sem,
    recv_sem,
):
    me = lax.axis_index("dom")
    barrier = pltpu.get_barrier_semaphore()
    for g in range(GROUPS):
        pl.semaphore_signal(
            barrier,
            inc=1,
            device_id=(partner(me, g, length),),
            device_id_type=pl.DeviceIdType.MESH,
        )

    def partial_copy(step, g):
        return pltpu.make_async_remote_copy(
            src_ref=leaving.at[pl.ds(SLOTS * g, SLOTS)],
            dst_ref=table.at[pl.ds(OWN + SLOTS * g, SLOTS)],
            send_sem=send_sem.at[step, 0, g],
            recv_sem=recv_sem.at[step, 0, g],
            device_id=(partner(me, g, length),),
            device_id_type=pl.DeviceIdType.MESH,
        )

    def speed_copy(step, g):
        return pltpu.make_async_remote_copy(
            src_ref=speed_out.at[pl.ds(3 * g, 3)],
            dst_ref=speed_in.at[pl.ds(3 * g, 3)],
            send_sem=send_sem.at[step, 1, g],
            recv_sem=recv_sem.at[step, 1, g],
            device_id=(partner(me, g, length),),
            device_id_type=pl.DeviceIdType.MESH,
        )

    row_id = lax.broadcasted_iota(jnp.int32, (8, 128), 0)
    lane_id = lax.broadcasted_iota(jnp.int32, (8, 128), 1)
    upper = row_id < 4
    left = lane_id < 64
    diagonal = upper == left
    upper_left = upper & left
    lower_right = diagonal & ~upper
    channel = row_id % 4
    zero_tile = jnp.zeros((8, 128), jnp.float32)

    ones = jnp.where((row_id == 0) | (row_id == 4), 1.0, 0.0)

    def load_tile(t, carry):
        lanes = pl.ds(pl.multiple_of(128 * t, 128), 128)
        spot = pl.ds(pl.multiple_of(8 * t, 8), 8)
        move[spot, :] = jnp.concatenate(
            [offset_in[:, lanes], velocity_in[:, lanes], zero_tile[0:2]], axis=0
        )
        affine8[spot, :] = affine_in[0:8, lanes]
        deform8[spot, :] = strain_in[0:8, lanes] + ones
        ninth[spot, :] = jnp.concatenate(
            [affine_in[8:9, lanes], strain_in[8:9, lanes] + 1.0, zero_tile[0:6]], axis=0
        )
        part_b[spot, :] = zero_tile
        part_c[spot, :] = zero_tile
        part_d[spot, :] = zero_tile
        spots_b[spot, :] = zero_tile
        return carry

    lax.fori_loop(0, TILES, load_tile, 0, unroll=4)
    plastic[...] = plastic_in[...]
    table[NONE] = zero_tile
    padded[NONE] = zero_tile

    def one_step(step, carry):
        def particles(r, carry):
            band = pl.ds(pl.multiple_of(8 * r, 8), 8)

            def every(i):
                return pl.ds(64 * r + i, 8, stride=8)

            f = [deform8[every(k), :] for k in range(8)] + [ninth[every(1), :]]
            volume = determinant(f)
            clamped = jnp.clip(volume, 1.0 - COMPRESS, 1.0 + STRETCH)
            hardened = plastic[band, :] * volume / clamped
            factor = jnp.exp(jnp.log(clamped / volume) / 3.0)
            e = [x * factor for x in f]
            for k in range(9):
                elastic[k, band, :] = e[k]
            elastic[9, band, :] = hardened
            live = live_in[band, :] != 0
            mass = jnp.where(live, mass_in[band, :], 0.0)
            stiff = jnp.exp(HARDEN * (1.0 - hardened))
            shear = SHEAR * stiff
            bulk = BULK * stiff * jnp.log(clamped)
            part_a[every(0), :] = mass
            part_a[every(4), :] = mass
            for i in range(3):
                value = mass * move[every(3 + i), :]
                part_a[every(1 + i), :] = value
                part_a[every(5 + i), :] = value
            inner = {}
            for i in range(3):
                for j in range(i, 3):
                    total = (
                        e[3 * i] * e[3 * j]
                        + e[3 * i + 1] * e[3 * j + 1]
                        + e[3 * i + 2] * e[3 * j + 2]
                    )
                    stress = shear * (total - 1.0) + bulk if i == j else shear * total
                    inner[i, j] = inner[j, i] = stress
            for i in range(3):
                for j, target in enumerate((part_b, part_c, part_d)):
                    k = 3 * i + j
                    affine = affine8[every(k), :] if k < 8 else ninth[every(0), :]
                    value = mass * (affine - (4.0 * DT) * inner[i, j])
                    value = jnp.where(live, value, 0.0)
                    target[every(1 + i), :] = value
                    target[every(5 + i), :] = value
            cell = cells[band, :]
            corner = (cell >> 4, (cell >> 2) & 3, cell & 3)
            spots = []
            for i in range(3):
                c = corner[i].astype(jnp.float32)
                frac = 0.5 + move[every(i), :]
                spots += [
                    c,
                    c + frac,
                    0.5 * (1.5 - frac) * (1.5 - frac),
                    0.75 - (frac - 1.0) * (frac - 1.0),
                    0.5 * (frac - 0.5) * (frac - 0.5),
                ]
            for k, value in enumerate(spots):
                if k < 8:
                    spots_a[every(k), :] = value
                else:
                    spots_b[every(k - 8), :] = value
            return carry

        lax.fori_loop(0, TILES // 8, particles, 0)

        def scatter(b, carry):
            mass_flow = pair(part_a, b)
            push = [pair(part_b, b), pair(part_c, b), pair(part_d, b)]
            tile_a = pair(spots_a, b)
            tile_b = pair(spots_b, b)
            lines = [tile_a[k : k + 1] for k in range(8)] + [tile_b[k : k + 1] for k in range(7)]
            first, second, third = lines[0:5], lines[5:10], lines[10:15]
            base = consts[80:88, :]
            base = jnp.concatenate([base, base], axis=1)
            blocks = [[], [], []]
            weights = []
            for a in range(3):
                node = base + float(a)
                w = weight(node, first)
                d = w * (node - first[1])
                weights.append((w, d))
                blocks[0].append(w * mass_flow + d * push[0])
                blocks[1].append(w * push[1])
                blocks[2].append(w * push[2])
            spot = pl.ds(pl.multiple_of(24 * b, 8), 24)
            first_w[spot, :] = jnp.concatenate([w for w, d in weights], axis=0)
            first_d[spot, :] = jnp.concatenate([d for w, d in weights], axis=0)
            lhs = jnp.concatenate([jnp.concatenate(x, axis=0) for x in blocks], axis=1)
            node2 = consts[0:40, :]
            node2 = jnp.concatenate([node2, node2], axis=1)
            node3 = consts[40:80, :]
            node3 = jnp.concatenate([node3, node3], axis=1)
            w23 = weight(node2, second) * weight(node3, third)
            rhs = jnp.concatenate(
                [w23, w23 * (node2 - second[1]), w23 * (node3 - third[1])], axis=1
            )
            rhs = jnp.concatenate([rhs, jnp.zeros((8, 3 * PMAX), jnp.float32)], axis=0)
            high = rhs.astype(jnp.bfloat16)
            low = low_part(rhs).astype(jnp.bfloat16)
            spot = pl.ds(pl.multiple_of(48 * b, 16), 48)
            weight_hi[spot, :] = high
            weight_lo[spot, :] = low
            lhs = high_low(lhs, 0)
            both = dot_nt(lhs, high) + dot_nt(lhs, low)
            total = both[0:24] + both[24:48]
            block = jnp.concatenate(
                [total[0:8, 0:36], total[8:16, 0:36], total[16:24, 0:36], zero_tile[:, 0:20]],
                axis=1,
            )
            own[b] = block
            table[b] = block
            return carry

        lax.fori_loop(0, OWN, scatter, 0, unroll=2)

        @pl.when(step == 0)
        def _():
            pl.semaphore_wait(barrier, GROUPS)

        for g in range(GROUPS):
            for k in range(SLOTS):
                leaving[SLOTS * g + k] = own[rows[SLOTS * g + k]]
            partial_copy(step, g).start()
        for g in range(GROUPS):
            partial_copy(step, g).wait()

        offset_id = consts[88:96, :]

        def collect(o, total):
            here = offset_id == o.astype(jnp.float32)
            return tuple(
                jnp.where(here, table[links[OWN * o + b]], total[b]) for b in range(OWN)
            )

        total = lax.fori_loop(0, 27, collect, (zero_tile,) * OWN)
        total = dot_nn(high_low(jnp.concatenate(total, axis=0), 1), gather_mat[...])
        for b in range(OWN):
            node = total[8 * b : 8 * b + 8]
            node = node + pltpu.roll(pltpu.roll(node, 4, 0), 64, 1)
            node = jnp.where(diagonal, node, 0.0)
            mass = jnp.where(channel == 0, node, 0.0)
            mass = mass + pltpu.roll(mass, 1, 0)
            mass = mass + pltpu.roll(mass, 2, 0)
            node = node / jnp.maximum(mass, MASS_FLOOR)
            node = node - jnp.where(channel == 3, DT * GRAVITY, 0.0)
            node = jnp.where(diagonal, node, 0.0)
            speed[b] = node
            speed_side[b] = pltpu.roll(node, 64, 1)

        for g in range(GROUPS):
            for m in range(3):
                r = [rows[SLOTS * g + 4 * m + k] for k in range(4)]
                speed_out[3 * g + m] = jnp.where(upper, speed[r[0]], speed[r[1]]) + jnp.where(
                    upper, speed_side[r[2]], speed_side[r[3]]
                )
            speed_copy(step, g).start()

        def spread(tiles):
            x = high_low(jnp.concatenate(tiles, axis=0), 1)
            return dot_nn(x, spread_mat[...]).reshape(len(tiles), 8, 128)

        padded[0:OWN] = spread([speed[b] for b in range(OWN)])
        for g in range(GROUPS):
            speed_copy(step, g).wait()
            tiles = []
            for m in range(3):
                z = speed_in[3 * g + m]
                zs = pltpu.roll(z, 4, 0)
                zl = pltpu.roll(z, 64, 1)
                zd = pltpu.roll(zs, 64, 1)
                tiles.append(jnp.where(upper_left, z, jnp.where(lower_right, zd, 0.0)))
                tiles.append(jnp.where(upper_left, zd, jnp.where(lower_right, z, 0.0)))
                tiles.append(jnp.where(upper_left, zl, jnp.where(lower_right, zs, 0.0)))
                tiles.append(jnp.where(upper_left, zs, jnp.where(lower_right, zl, 0.0)))
            padded[OWN + SLOTS * g : OWN + SLOTS * g + SLOTS] = spread(tiles)

        def fetch(o, total):
            here = offset_id == (26 - o).astype(jnp.float32)
            return tuple(
                jnp.where(here, padded[links[OWN * o + b]], total[b]) for b in range(OWN)
            )

        total = lax.fori_loop(0, 27, fetch, (zero_tile,) * OWN)
        for b in range(OWN):
            field[b] = total[b]

        upper_wide = lax.broadcasted_iota(jnp.int32, (8, PMAX), 0) < 4

        def gather(b, carry):
            v = field[b]
            v = jnp.concatenate([v[:, 0:48], v[:, 36:84], v[:, 72:120]], axis=0)
            v = high_low(v, 0)
            spot = pl.ds(pl.multiple_of(48 * b, 16), 48)
            both = dot_nn(v, weight_hi[spot, :]) + dot_nn(v, weight_lo[spot, :])
            result = both[0:24] + both[24:48]
            spot = pl.ds(pl.multiple_of(24 * b, 8), 24)

            def fold(x):
                x = x[0:8] + x[8:16] + x[16:24]
                return x + pltpu.roll(x, 4, 0)

            w = first_w[spot, :]
            plain = fold(w * result[:, 0:PMAX])
            by1 = fold(first_d[spot, :] * result[:, 0:PMAX])
            by2 = fold(w * result[:, PMAX : 2 * PMAX])
            by3 = fold(w * result[:, 2 * PMAX : 3 * PMAX])
            spot = pl.ds(pl.multiple_of(16 * b, 16), 16)
            out = jnp.where(upper_wide, plain, by1)
            found_a[spot, :] = jnp.concatenate([out[:, 0:128], out[:, 128:256]], axis=0)
            out = jnp.where(upper_wide, by2, by3)
            found_b[spot, :] = jnp.concatenate([out[:, 0:128], out[:, 128:256]], axis=0)
            return carry

        lax.fori_loop(0, OWN, gather, 0, unroll=2)

        def finish(r, carry):
            band = pl.ds(pl.multiple_of(8 * r, 8), 8)

            def every(i):
                return pl.ds(64 * r + i, 8, stride=8)

            live = live_in[band, :] != 0

            def put(ref, i, value):
                ref[every(i), :] = jnp.where(live, value, ref[every(i), :])

            v = [found_a[every(1 + i), :] for i in range(3)]
            moment = [
                [found_a[every(5 + i), :] for i in range(3)],
                [found_b[every(1 + i), :] for i in range(3)],
                [found_b[every(5 + i), :] for i in range(3)],
            ]
            affine = [4.0 * moment[j][i] for i in range(3) for j in range(3)]
            e = [elastic[k, band, :] for k in range(9)]
            for i in range(3):
                put(move, i, move[every(i), :] + DT * v[i])
                put(move, 3 + i, v[i])
            for i in range(3):
                for j in range(3):
                    k = 3 * i + j
                    total = e[k]
                    for m in range(3):
                        total = total + DT * affine[3 * i + m] * e[3 * m + j]
                    if k < 8:
                        put(affine8, k, affine[k])
                        put(deform8, k, total)
                    else:
                        put(ninth, 0, affine[k])
                        put(ninth, 1, total)
            plastic[band, :] = jnp.where(live, elastic[9, band, :], plastic[band, :])
            return carry

        lax.fori_loop(0, TILES // 8, finish, 0)
        return carry

    lax.fori_loop(0, 2, one_step, 0)

    def store_tile(t, carry):
        lanes = pl.ds(pl.multiple_of(128 * t, 128), 128)
        spot = pl.ds(pl.multiple_of(8 * t, 8), 8)
        value = move[spot, :]
        offset_out[:, lanes] = value[0:3]
        velocity_out[:, lanes] = value[3:6]
        affine_out[0:8, lanes] = affine8[spot, :]
        deform_out[0:8, lanes] = deform8[spot, :]
        value = ninth[spot, :]
        affine_out[8:9, lanes] = value[0:1]
        deform_out[8:9, lanes] = value[1:2]
        return carry

    lax.fori_loop(0, TILES, store_tile, 0, unroll=4)
    plastic_out[...] = plastic[...]


def on_device(
    length,
    base_cell,
    offset,
    velocity,
    affine,
    strain,
    plastic,
    particle_mass,
    counts,
    neighbours,
    send_rows,
):
    me = lax.axis_index("dom")
    remote = jnp.maximum(neighbours - OWN, 0)
    group = remote // SLOTS
    source = jnp.where(group < HOPS, me - (group + 1), me + (group - HOPS + 1))
    present = (neighbours >= 0) & ((neighbours < OWN) | ((source >= 0) & (source < length)))
    links = jnp.where(present, neighbours, NONE).T.reshape(-1)
    slot = jnp.arange(PMAX, dtype=jnp.int32)[None, :]
    live = (slot < counts[:, None]).astype(jnp.int32).reshape(TILES, 128)
    consts, gather_mat, spread_mat = tables()
    vmem = pl.BlockSpec(memory_space=pltpu.VMEM)
    smem = pl.BlockSpec(memory_space=pltpu.SMEM)
    f32 = jnp.float32
    tile = pltpu.VMEM((8 * TILES, 128), f32)
    planar = (TILES, 128)
    outs = pl.pallas_call(
        lambda *refs: step_kernel(length, *refs),
        out_shape=(
            jax.ShapeDtypeStruct((3, PARTICLES), f32),
            jax.ShapeDtypeStruct((3, PARTICLES), f32),
            jax.ShapeDtypeStruct((9, PARTICLES), f32),
            jax.ShapeDtypeStruct((9, PARTICLES), f32),
            jax.ShapeDtypeStruct(planar, f32),
        ),
        in_specs=[smem, smem] + [vmem] * 11,
        out_specs=(vmem,) * 5,
        scratch_shapes=[
            tile,
            tile,
            tile,
            tile,
            pltpu.VMEM(planar, f32),
            pltpu.VMEM((10,) + planar, f32),
            tile,
            tile,
            tile,
            tile,
            tile,
            tile,
            pltpu.VMEM((48 * OWN, 3 * PMAX), jnp.bfloat16),
            pltpu.VMEM((48 * OWN, 3 * PMAX), jnp.bfloat16),
            pltpu.VMEM((24 * OWN, PMAX), f32),
            pltpu.VMEM((24 * OWN, PMAX), f32),
            pltpu.VMEM((OWN, 8, 128), f32),
            pltpu.VMEM((NONE + 1, 8, 128), f32),
            pltpu.VMEM((RECEIVED, 8, 128), f32),
            pltpu.VMEM((OWN, 8, 128), f32),
            pltpu.VMEM((OWN, 8, 128), f32),
            pltpu.VMEM((3 * GROUPS, 8, 128), f32),
            pltpu.VMEM((3 * GROUPS, 8, 128), f32),
            pltpu.VMEM((NONE + 1, 8, 128), f32),
            pltpu.VMEM((OWN, 8, 128), f32),
            tile,
            tile,
            pltpu.SemaphoreType.DMA((2, 2, GROUPS)),
            pltpu.SemaphoreType.DMA((2, 2, GROUPS)),
        ],
        compiler_params=pltpu.CompilerParams(
            collective_id=0, has_side_effects=True, vmem_limit_bytes=40 * 1024 * 1024
        ),
        name="snow_steps",
    )(
        links,
        send_rows.reshape(-1),
        base_cell.reshape(planar),
        offset,
        velocity,
        affine,
        strain,
        plastic.reshape(planar),
        particle_mass.reshape(planar),
        live,
        jnp.asarray(consts),
        jnp.asarray(gather_mat, dtype=jnp.bfloat16),
        jnp.asarray(spread_mat, dtype=jnp.bfloat16),
    )
    return outs[:4] + (outs[4].reshape(PARTICLES),)


def solution(mesh):
    length = mesh.shape["dom"]
    wide = P(None, "dom")
    flat = P("dom")
    return jax.shard_map(
        lambda *args: on_device(length, *args),
        mesh=mesh,
        in_specs=(flat, wide, wide, wide, wide, flat, flat, flat, P("dom", None), P("dom", None)),
        out_specs=(wide, wide, wide, wide, flat),
        check_vma=False,
    )
```

time: 215 us -> 72.7 us (0.34)
  the two profiles are of different devices: /device:TPU:32 before, /device:TPU:1 now
where the time goes in v1:
time: 72.7 us; the launch traced here: 72.2 us
  Pallas kernels  60 us (83%)
  local copies, waits for them, and re-layouts  11.4 us (16%)
    pallas_call x1, Pallas kernels, on_device(): pl.pallas_call(lambda *refs: step_kernel(length, *refs), out_shape=(jax.S...  60 us
    unnamed x31, local copies, waits for them, and re-layouts  11 us

profile of v1, /device:TPU:1, one launch (start us, length us, event | category | flops | bytes accessed | tf_op | source)
XLA Modules:
  0.0 72.2 jit_solution(8859622576952552785)
XLA Ops:
  0.6 0.0 copy-start.11
  0.6 0.0 copy-start.12
  0.7 0.0 copy-start.2
  0.7 0.0 copy-start.3
  0.7 0.6 copy-done.11
  1.4 0.1 copy.18
  1.4 0.1 reshape.33.refs_0_
  1.5 0.0 copy-done.12
  1.5 0.1 lt.47
  1.6 0.1 lt.48
  1.7 0.0 copy-start.10
  1.7 0.1 compare_convert_fusion.refs_9_
  1.8 0.0 copy-done.2
  1.8 0.0 copy-done.3
  1.8 0.6 copy-done.10
  2.4 0.0 copy-start
  2.4 0.9 %copy-done = f32[9,4096]{1,0:T(8,128)S(1)} copy-done((f32[9,4096]{1,0:T(8,128)S(1)}, f32[9,4096]{1,0:T(8,128)}, u32[]{:S(2)}) %copy-start) | copy-done | bytes 147480
  3.3 0.0 copy-start.1
  3.3 0.9 %copy-done.1 = f32[9,4096]{1,0:T(8,128)S(1)} copy-done((f32[9,4096]{1,0:T(8,128)S(1)}, f32[9,4096]{1,0:T(8,128)}, u32[]{:S(2)}) %copy-start.1) | copy-done | bytes 147480
  4.3 0.0 copy-start.4
  4.3 0.8 %copy-done.4 = bf16[256,128]{1,0:T(8,128)(2,1)S(1)} copy-done((bf16[256,128]{1,0:T(8,128)(2,1)S(1)}, bf16[256,128]{1,0:T(8,128)(2,1)}, u32[]{:S(2)}) %copy-start.4) | copy-done | bytes 65560
  5.1 0.8 %copy-done.5 = bf16[256,128]{1,0:T(8,128)(2,1)S(1)} copy-done((bf16[256,128]{1,0:T(8,128)(2,1)S(1)}, bf16[256,128]{1,0:T(8,128)(2,1)}, u32[]{:S(2)}) %copy-start.5) | copy-done | bytes 65560
  5.9 0.8 %copy-done.6 = f32[96,128]{1,0:T(8,128)S(1)} copy-done((f32[96,128]{1,0:T(8,128)S(1)}, f32[96,128]{1,0:T(8,128)}, u32[]{:S(2)}) %copy-start.6) | copy-done | bytes 49176
  6.7 0.7 copy-done.7
  7.5 0.7 copy-done.8
  8.2 0.7 copy-done.9
  8.9 60.0 %snow_steps.1 = (f32[3,4096]{1,0:T(4,128)S(1)}, f32[3,4096]{1,0:T(4,128)S(1)}, f32[9,4096]{1,0:T(8,128)S(1)}, f32[9,4096]{1,0:T(8,128)S(1)}, f32[32,128]{1,0:T(8,128)S(1)}) custom-call(s32[432]{0:T(512)S(1)} %reshape.33.refs_0_, s32[96]{0:T(128)S(1)} %bitcast.12, s32[32,128]{1,0:T(8,128)S(1)} %bitcast.8, f32[3,4096]{1,0:T(4,128)S(1)} %copy-done.2, ...), custom_call_target="tpu_custom_call" | custom-call | tf_op jit(solution)/shard_map/snow_steps/pallas_call | solution.py:520
  68.9 0.6 copy.24
  69.5 0.6 copy.25
  70.2 0.7 copy.26
  70.9 0.7 copy.27
  71.6 0.6 copy.28
  (8 shorter events, 0.0 us)
Async XLA Ops:
  0.6 0.7 copy-start.11
  0.6 0.9 %copy-start.12 = (s32[16]{0:T(128)S(1)}, s32[16]{0:T(128)}, u32[]{:S(2)}) copy-start(s32[16]{0:T(128)} %param.20) | copy-start | bytes 196
  0.7 1.1 %copy-start.2 = (f32[3,4096]{1,0:T(4,128)S(1)}, f32[3,4096]{1,0:T(4,128)}, u32[]{:S(2)}) copy-start(f32[3,4096]{1,0:T(4,128)} %refs_3_.1) | copy-start | bytes 147460
  0.7 1.1 %copy-start.3 = (f32[3,4096]{1,0:T(4,128)S(1)}, f32[3,4096]{1,0:T(4,128)}, u32[]{:S(2)}) copy-start(f32[3,4096]{1,0:T(4,128)} %refs_4_.1) | copy-start | bytes 147460
  1.7 0.7 copy-start.10
  2.4 0.9 %copy-start = (f32[9,4096]{1,0:T(8,128)S(1)}, f32[9,4096]{1,0:T(8,128)}, u32[]{:S(2)}) copy-start(f32[9,4096]{1,0:T(8,128)} %refs_5_.1) | copy-start | bytes 442372
  3.3 0.9 %copy-start.1 = (f32[9,4096]{1,0:T(8,128)S(1)}, f32[9,4096]{1,0:T(8,128)}, u32[]{:S(2)}) copy-start(f32[9,4096]{1,0:T(8,128)} %refs_6_.1) | copy-start | bytes 442372
  4.3 0.8 %copy-start.4 = (bf16[256,128]{1,0:T(8,128)(2,1)S(1)}, bf16[256,128]{1,0:T(8,128)(2,1)}, u32[]{:S(2)}) copy-start(bf16[256,128]{1,0:T(8,128)(2,1)} %constant.40.clone.refs_12_) | copy-start | bytes 196612
  5.1 0.8 %copy-start.5 = (bf16[256,128]{1,0:T(8,128)(2,1)S(1)}, bf16[256,128]{1,0:T(8,128)(2,1)}, u32[]{:S(2)}) copy-start(bf16[256,128]{1,0:T(8,128)(2,1)} %constant.39.clone.refs_11_) | copy-start | bytes 196612
  5.9 0.8 %copy-start.6 = (f32[96,128]{1,0:T(8,128)S(1)}, f32[96,128]{1,0:T(8,128)}, u32[]{:S(2)}) copy-start(f32[96,128]{1,0:T(8,128)} %constant.38.clone.refs_10_) | copy-start | bytes 147460
  6.7 0.7 copy-start.7
  7.5 0.7 copy-start.8
  8.2 0.7 copy-start.9

commit v2 on v1

--- a/solution.py
+++ b/solution.py
@@ -12,7 +12,7 @@
 SLOTS = 12
 GROUPS = 2 * HOPS
 RECEIVED = GROUPS * SLOTS
-NONE = OWN + RECEIVED
+TABLE = 1 + OWN + RECEIVED
 PARTICLES = OWN * PMAX
 TILES = PARTICLES // 128
 
@@ -53,9 +53,8 @@
             offset_id,
         ]
     ).astype(np.float32)
-    gather = np.concatenate([fold, fold])
-    spread = np.concatenate([fold.T, fold.T])
-    return consts, gather, spread
+    folds = np.stack([np.concatenate([fold, fold]), np.concatenate([fold.T, fold.T])])
+    return consts, folds
 
 
 def determinant(m):
@@ -100,56 +99,57 @@
     return lax.rem(me + (by + length), length)
 
 
-def step_kernel(
-    length,
-    links,
-    rows,
-    cells,
-    offset_in,
-    velocity_in,
-    affine_in,
-    strain_in,
-    plastic_in,
-    mass_in,
-    live_in,
-    consts,
-    gather_mat,
-    spread_mat,
-    offset_out,
-    velocity_out,
-    affine_out,
-    deform_out,
-    plastic_out,
-    move,
-    affine8,
-    deform8,
-    ninth,
-    plastic,
-    elastic,
-    part_a,
-    part_b,
-    part_c,
-    part_d,
-    spots_a,
-    spots_b,
-    weight_hi,
-    weight_lo,
-    first_w,
-    first_d,
-    own,
-    table,
-    leaving,
-    speed,
-    speed_side,
-    speed_out,
-    speed_in,
-    padded,
-    field,
-    found_a,
-    found_b,
-    send_sem,
-    recv_sem,
-):
+def step_kernel(length, *refs):
+    given, results, held, work = refs[0:12], refs[12:17], refs[17:29], refs[29:]
+    (
+        links,
+        rows,
+        counts,
+        cells,
+        offset_in,
+        velocity_in,
+        affine_in,
+        strain_in,
+        plastic_in,
+        mass_in,
+        consts,
+        fold_mats,
+    ) = held
+    offset_out, velocity_out, affine_out, deform_out, plastic = results
+    (
+        move,
+        affine8,
+        deform8,
+        ninth,
+        elastic,
+        part_a,
+        part_b,
+        part_c,
+        part_d,
+        spots_a,
+        spots_b,
+        weight_hi,
+        weight_lo,
+        first_w,
+        first_d,
+        own,
+        table,
+        leaving,
+        speed,
+        speed_side,
+        speed_out,
+        speed_in,
+        padded,
+        field,
+        found_a,
+        found_b,
+        send_sem,
+        recv_sem,
+        load_sem,
+    ) = work
+    loads = [pltpu.make_async_copy(given[k], held[k], load_sem.at[k]) for k in range(12)]
+    for copy in loads:
+        copy.start()
     me = lax.axis_index("dom")
     barrier = pltpu.get_barrier_semaphore()
     for g in range(GROUPS):
@@ -163,7 +163,7 @@
     def partial_copy(step, g):
         return pltpu.make_async_remote_copy(
             src_ref=leaving.at[pl.ds(SLOTS * g, SLOTS)],
-            dst_ref=table.at[pl.ds(OWN + SLOTS * g, SLOTS)],
+            dst_ref=table.at[pl.ds(1 + OWN + SLOTS * g, SLOTS)],
             send_sem=send_sem.at[step, 0, g],
             recv_sem=recv_sem.at[step, 0, g],
             device_id=(partner(me, g, length),),
@@ -180,6 +180,15 @@
             device_id_type=pl.DeviceIdType.MESH,
         )
 
+    def drop_outside(ref, g):
+        source = me - (g + 1) if g < HOPS else me + (g - HOPS + 1)
+
+        @pl.when((source < 0) | (source >= length))
+        def _():
+            ref[1 + OWN + SLOTS * g : 1 + OWN + SLOTS * (g + 1)] = jnp.zeros(
+                (SLOTS, 8, 128), jnp.float32
+            )
+
     row_id = lax.broadcasted_iota(jnp.int32, (8, 128), 0)
     lane_id = lax.broadcasted_iota(jnp.int32, (8, 128), 1)
     upper = row_id < 4
@@ -189,6 +198,14 @@
     lower_right = diagonal & ~upper
     channel = row_id % 4
     zero_tile = jnp.zeros((8, 128), jnp.float32)
+
+    slot = lane_id + 128 * (row_id % 2)
+
+    def live_slots(r):
+        limit = counts[4 * r + 3]
+        for k in (2, 1, 0):
+            limit = jnp.where(row_id < 2 * k + 2, counts[4 * r + k], limit)
+        return slot < limit
 
     ones = jnp.where((row_id == 0) | (row_id == 4), 1.0, 0.0)
 
@@ -209,10 +226,12 @@
         spots_b[spot, :] = zero_tile
         return carry
 
+    for copy in loads:
+        copy.wait()
     lax.fori_loop(0, TILES, load_tile, 0, unroll=4)
     plastic[...] = plastic_in[...]
-    table[NONE] = zero_tile
-    padded[NONE] = zero_tile
+    table[0] = zero_tile
+    padded[0] = zero_tile
 
     def one_step(step, carry):
         def particles(r, carry):
@@ -230,7 +249,7 @@
             for k in range(9):
                 elastic[k, band, :] = e[k]
             elastic[9, band, :] = hardened
-            live = live_in[band, :] != 0
+            live = live_slots(r)
             mass = jnp.where(live, mass_in[band, :], 0.0)
             stiff = jnp.exp(HARDEN * (1.0 - hardened))
             shear = SHEAR * stiff
@@ -326,10 +345,10 @@
                 axis=1,
             )
             own[b] = block
-            table[b] = block
+            table[1 + b] = block
             return carry
 
-        lax.fori_loop(0, OWN, scatter, 0, unroll=2)
+        lax.fori_loop(0, OWN, scatter, 0, unroll=8)
 
         @pl.when(step == 0)
         def _():
@@ -337,21 +356,22 @@
 
         for g in range(GROUPS):
             for k in range(SLOTS):
-                leaving[SLOTS * g + k] = own[rows[SLOTS * g + k]]
+                leaving[SLOTS * g + k] = own[rows[0, SLOTS * g + k]]
             partial_copy(step, g).start()
         for g in range(GROUPS):
             partial_copy(step, g).wait()
+            drop_outside(table, g)
 
         offset_id = consts[88:96, :]
 
         def collect(o, total):
             here = offset_id == o.astype(jnp.float32)
             return tuple(
-                jnp.where(here, table[links[OWN * o + b]], total[b]) for b in range(OWN)
+                jnp.where(here, table[1 + links[b, o]], total[b]) for b in range(OWN)
             )
 
         total = lax.fori_loop(0, 27, collect, (zero_tile,) * OWN)
-        total = dot_nn(high_low(jnp.concatenate(total, axis=0), 1), gather_mat[...])
+        total = dot_nn(high_low(jnp.concatenate(total, axis=0), 1), fold_mats[0])
         for b in range(OWN):
             node = total[8 * b : 8 * b + 8]
             node = node + pltpu.roll(pltpu.roll(node, 4, 0), 64, 1)
@@ -367,7 +387,7 @@
 
         for g in range(GROUPS):
             for m in range(3):
-                r = [rows[SLOTS * g + 4 * m + k] for k in range(4)]
+                r = [rows[0, SLOTS * g + 4 * m + k] for k in range(4)]
                 speed_out[3 * g + m] = jnp.where(upper, speed[r[0]], speed[r[1]]) + jnp.where(
                     upper, speed_side[r[2]], speed_side[r[3]]
                 )
@@ -375,9 +395,9 @@
 
         def spread(tiles):
             x = high_low(jnp.concatenate(tiles, axis=0), 1)
-            return dot_nn(x, spread_mat[...]).reshape(len(tiles), 8, 128)
-
-        padded[0:OWN] = spread([speed[b] for b in range(OWN)])
+            return dot_nn(x, fold_mats[1]).reshape(len(tiles), 8, 128)
+
+        padded[1 : 1 + OWN] = spread([speed[b] for b in range(OWN)])
         for g in range(GROUPS):
             speed_copy(step, g).wait()
             tiles = []
@@ -390,12 +410,13 @@
                 tiles.append(jnp.where(upper_left, zd, jnp.where(lower_right, z, 0.0)))
                 tiles.append(jnp.where(upper_left, zl, jnp.where(lower_right, zs, 0.0)))
                 tiles.append(jnp.where(upper_left, zs, jnp.where(lower_right, zl, 0.0)))
-            padded[OWN + SLOTS * g : OWN + SLOTS * g + SLOTS] = spread(tiles)
+            padded[1 + OWN + SLOTS * g : 1 + OWN + SLOTS * (g + 1)] = spread(tiles)
+            drop_outside(padded, g)
 
         def fetch(o, total):
             here = offset_id == (26 - o).astype(jnp.float32)
             return tuple(
-                jnp.where(here, padded[links[OWN * o + b]], total[b]) for b in range(OWN)
+                jnp.where(here, padded[1 + links[b, o]], total[b]) for b in range(OWN)
             )
 
         total = lax.fori_loop(0, 27, fetch, (zero_tile,) * OWN)
@@ -429,7 +450,7 @@
             found_b[spot, :] = jnp.concatenate([out[:, 0:128], out[:, 128:256]], axis=0)
             return carry
 
-        lax.fori_loop(0, OWN, gather, 0, unroll=2)
+        lax.fori_loop(0, OWN, gather, 0, unroll=8)
 
         def finish(r, carry):
             band = pl.ds(pl.multiple_of(8 * r, 8), 8)
@@ -437,7 +458,7 @@
             def every(i):
                 return pl.ds(64 * r + i, 8, stride=8)
 
-            live = live_in[band, :] != 0
+            live = live_slots(r)
 
             def put(ref, i, value):
                 ref[every(i), :] = jnp.where(live, value, ref[every(i), :])
@@ -487,7 +508,21 @@
         return carry
 
     lax.fori_loop(0, TILES, store_tile, 0, unroll=4)
-    plastic_out[...] = plastic[...]
+
+
+def hand_over(*refs):
+    first, last, held = refs[0:5], refs[5:10], refs[10:15]
+    copies = []
+    for k in range(5):
+        come = pltpu.make_async_copy(first[k], held[k], refs[15].at[0, k])
+        leave = pltpu.make_async_copy(held[k], last[k], refs[15].at[1, k])
+        copies.append((come, leave))
+        come.start()
+    for come, leave in copies:
+        come.wait()
+        leave.start()
+    for come, leave in copies:
+        leave.wait()
 
 
 def on_device(
@@ -503,37 +538,38 @@
     neighbours,
     send_rows,
 ):
-    me = lax.axis_index("dom")
-    remote = jnp.maximum(neighbours - OWN, 0)
-    group = remote // SLOTS
-    source = jnp.where(group < HOPS, me - (group + 1), me + (group - HOPS + 1))
-    present = (neighbours >= 0) & ((neighbours < OWN) | ((source >= 0) & (source < length)))
-    links = jnp.where(present, neighbours, NONE).T.reshape(-1)
-    slot = jnp.arange(PMAX, dtype=jnp.int32)[None, :]
-    live = (slot < counts[:, None]).astype(jnp.int32).reshape(TILES, 128)
-    consts, gather_mat, spread_mat = tables()
+    consts, folds = tables()
+    hbm = pl.BlockSpec(memory_space=pltpu.HBM)
     vmem = pl.BlockSpec(memory_space=pltpu.VMEM)
-    smem = pl.BlockSpec(memory_space=pltpu.SMEM)
     f32 = jnp.float32
+    i32 = jnp.int32
     tile = pltpu.VMEM((8 * TILES, 128), f32)
     planar = (TILES, 128)
+    row3 = (3, PARTICLES)
+    row9 = (9, PARTICLES)
+    shapes = [jax.ShapeDtypeStruct(x, f32) for x in (row3, row3, row9, row9, planar)]
     outs = pl.pallas_call(
         lambda *refs: step_kernel(length, *refs),
-        out_shape=(
-            jax.ShapeDtypeStruct((3, PARTICLES), f32),
-            jax.ShapeDtypeStruct((3, PARTICLES), f32),
-            jax.ShapeDtypeStruct((9, PARTICLES), f32),
-            jax.ShapeDtypeStruct((9, PARTICLES), f32),
-            jax.ShapeDtypeStruct(planar, f32),
-        ),
-        in_specs=[smem, smem] + [vmem] * 11,
-        out_specs=(vmem,) * 5,
+        out_shape=shapes,
+        in_specs=[hbm] * 12,
+        out_specs=[vmem] * 5,
         scratch_shapes=[
-            tile,
-            tile,
-            tile,
-            tile,
+            pltpu.SMEM((OWN, 27), i32),
+            pltpu.SMEM((1, RECEIVED), i32),
+            pltpu.SMEM((OWN,), i32),
+            pltpu.VMEM(planar, i32),
+            pltpu.VMEM(row3, f32),
+            pltpu.VMEM(row3, f32),
+            pltpu.VMEM(row9, f32),
+            pltpu.VMEM(row9, f32),
             pltpu.VMEM(planar, f32),
+            pltpu.VMEM(planar, f32),
+            pltpu.VMEM((96, 128), f32),
+            pltpu.VMEM((2, 256, 128), jnp.bfloat16),
+            tile,
+            tile,
+            tile,
+            tile,
             pltpu.VMEM((10,) + planar, f32),
             tile,
             tile,
@@ -546,26 +582,28 @@
             pltpu.VMEM((24 * OWN, PMAX), f32),
             pltpu.VMEM((24 * OWN, PMAX), f32),
             pltpu.VMEM((OWN, 8, 128), f32),
-            pltpu.VMEM((NONE + 1, 8, 128), f32),
+            pltpu.VMEM((TABLE, 8, 128), f32),
             pltpu.VMEM((RECEIVED, 8, 128), f32),
             pltpu.VMEM((OWN, 8, 128), f32),
             pltpu.VMEM((OWN, 8, 128), f32),
             pltpu.VMEM((3 * GROUPS, 8, 128), f32),
             pltpu.VMEM((3 * GROUPS, 8, 128), f32),
-            pltpu.VMEM((NONE + 1, 8, 128), f32),
+            pltpu.VMEM((TABLE, 8, 128), f32),
             pltpu.VMEM((OWN, 8, 128), f32),
             tile,
             tile,
             pltpu.SemaphoreType.DMA((2, 2, GROUPS)),
             pltpu.SemaphoreType.DMA((2, 2, GROUPS)),
+            pltpu.SemaphoreType.DMA((12,)),
         ],
         compiler_params=pltpu.CompilerParams(
-            collective_id=0, has_side_effects=True, vmem_limit_bytes=40 * 1024 * 1024
+            collective_id=0, has_side_effects=True, vmem_limit_bytes=62 * 1024 * 1024
         ),
         name="snow_steps",
     )(
-        links,
-        send_rows.reshape(-1),
+        neighbours,
+        send_rows,
+        counts,
         base_cell.reshape(planar),
         offset,
         velocity,
@@ -573,12 +611,19 @@
         strain,
         plastic.reshape(planar),
         particle_mass.reshape(planar),
-        live,
         jnp.asarray(consts),
-        jnp.asarray(gather_mat, dtype=jnp.bfloat16),
-        jnp.asarray(spread_mat, dtype=jnp.bfloat16),
+        jnp.asarray(folds, dtype=jnp.bfloat16),
     )
-    return outs[:4] + (outs[4].reshape(PARTICLES),)
+    outs = pl.pallas_call(
+        hand_over,
+        out_shape=shapes,
+        in_specs=[hbm] * 5,
+        out_specs=[hbm] * 5,
+        scratch_shapes=[pltpu.VMEM(x.shape, f32) for x in shapes] + [pltpu.SemaphoreType.DMA((2, 5))],
+        compiler_params=pltpu.CompilerParams(vmem_limit_bytes=62 * 1024 * 1024),
+        name="hand_over",
+    )(*outs)
+    return tuple(outs[:4]) + (outs[4].reshape(PARTICLES),)
 
 
 def solution(mesh):

time: 72.7 us -> 59.9 us (0.82)
  local copies, waits for them, and re-layouts: 11.4 us -> 0 us
  Pallas kernels: 60 us -> 59.1 us
    unnamed x31 -> x0, local copies, waits for them, and re-layouts: 11 us -> none
    pallas_call x1 -> x2, Pallas kernels: 60 us -> 59.1 us  [the longest x1 57.2 us: on_device(): pl.pallas_call(lambda *refs: step_kernel(length, *refs), out_shape=shapes...]
where the time goes in v2:
time: 59.9 us; the launch traced here: 59.7 us
  Pallas kernels  59.1 us (99%)
  between operations  0.64 us (1%)
    pallas_call x1, Pallas kernels, on_device(): pl.pallas_call(lambda *refs: step_kernel(length, *refs), out_shape=shapes...  57.2 us
    pallas_call x1, Pallas kernels, on_device(): pl.pallas_call(hand_over, out_shape=shapes, in_specs=[hbm] * 5, out_specs...  1.91 us

profile of v2, /device:TPU:1, one launch (start us, length us, event | category | flops | bytes accessed | tf_op | source)
XLA Modules:
  0.0 59.7 jit_solution(13091964679831035816)
XLA Ops:
  0.6 57.2 %snow_steps.1 = (f32[3,4096]{1,0:T(4,128)}, f32[3,4096]{1,0:T(4,128)}, f32[9,4096]{1,0:T(8,128)}, f32[9,4096]{1,0:T(8,128)}, f32[32,128]{1,0:T(8,128)}) custom-call(s32[16,27]{1,0:T(8,128)} %refs_0_.1, s32[1,96]{1,0:T(1,128)} %refs_1_.1, s32[16]{0:T(128)} %refs_2_.1, s32[32,128]{1,0:T(8,128)} %bitcast.4, f32[3,4096]{1,0:T(4,128)} %refs_4_.1, ...), custom_call_target="tpu_custom_call" | custom-call | tf_op jit(solution)/shard_map/snow_steps/pallas_call | solution.py:551
  57.8 1.9 %hand_over.1 = (f32[3,4096]{1,0:T(4,128)}, f32[3,4096]{1,0:T(4,128)}, f32[9,4096]{1,0:T(8,128)}, f32[9,4096]{1,0:T(8,128)}, f32[32,128]{1,0:T(8,128)}) custom-call(f32[3,4096]{1,0:T(4,128)} %get-tuple-element.15.refs_0_, f32[3,4096]{1,0:T(4,128)} %get-tuple-element.16.refs_1_, f32[9,4096]{1,0:T(8,128)} %get-tuple-element.17.refs_2_, ...), custom_call_target="tpu_custom_call" | custom-call | tf_op jit(solution)/shard_map/hand_over/pallas_call | solution.py:617

commit v3 on v2

--- a/solution.py
+++ b/solution.py
@@ -15,6 +15,11 @@
 TABLE = 1 + OWN + RECEIVED
 PARTICLES = OWN * PMAX
 TILES = PARTICLES // 128
+RIM = 20
+USED = 36 + 2 * RIM
+SENT = 8
+FAR_FIRST = (3, 7, 2, 6, 1, 5, 0, 4)
+NEAR_FIRST = (0, 4, 1, 5, 2, 6, 3, 7)
 
 DT = 0.05
 SHEAR = 4.0
@@ -27,13 +32,19 @@
 
 
 def tables():
-    row = np.arange(8)[:, None]
-    lane = np.arange(128)[None, :]
-    half = row // 4 + 0 * lane
-    third = lane // 36 + 0 * row
-    place = lane % 36 + 0 * row
+    places = [(j2, j3) for j2 in range(6) for j3 in range(6)]
+    places.sort(key=lambda x: (x[0] in (1, 2, 3, 4) and x[1] in (1, 2, 3, 4), x))
+    lanes = [(0, q) for q in range(36)]
+    lanes += [(a, q) for a in (1, 2) for q in range(RIM)]
+    lanes += [(a, q) for a in (1, 2) for q in range(RIM, 36)]
+    lanes += [(3, 0)] * 20
+    half = np.arange(8)[:, None] // 4 + np.zeros((1, 128), int)
+    third = np.array([x[0] for x in lanes])[None, :] + 0 * half
+    place = np.array([x[1] for x in lanes])[None, :] + 0 * half
     inside = third < 3
-    node = [3 * half + third, place // 6, place % 6]
+    spot2 = np.array([x[0] for x in places])
+    spot3 = np.array([x[1] for x in places])
+    node = [np.where(half == 0, third, 5 - third), spot2[place], spot3[place]]
     step = [(x == 0).astype(int) - (x == 5).astype(int) for x in node]
     offset_id = 9 * (step[0] + 1) + 3 * (step[1] + 1) + step[2] + 1
     offset_id = np.where(inside, offset_id, 13)
@@ -43,13 +54,15 @@
     for h in range(2):
         for l in range(108):
             fold[l, 64 * h + core_id[4 * h, l]] = 1.0
-    spot = np.arange(40)
     wide = np.zeros((40, 128))
+    none = [6] * 4
     consts = np.concatenate(
         [
-            wide + (spot // 6)[:, None],
-            wide + (spot % 6)[:, None],
-            3 * half,
+            wide + np.append(spot2, none)[:, None],
+            wide + np.append(spot3, none)[:, None],
+            np.where(half == 0, 0, 5),
+            np.where(half == 0, 1, 4),
+            np.where(half == 0, 2, 3),
             offset_id,
         ]
     ).astype(np.float32)
@@ -94,9 +107,12 @@
     return jnp.concatenate([both[0:8], both[8:16]], axis=1)
 
 
+def reach(group):
+    return group + 1 if group < HOPS else -(group - HOPS + 1)
+
+
 def partner(me, group, length):
-    by = group + 1 if group < HOPS else -(group - HOPS + 1)
-    return lax.rem(me + (by + length), length)
+    return lax.rem(me + (reach(group) + length), length)
 
 
 def step_kernel(length, *refs):
@@ -152,18 +168,43 @@
         copy.start()
     me = lax.axis_index("dom")
     barrier = pltpu.get_barrier_semaphore()
+
+    def receives(g):
+        return (me + reach(g) >= 0) & (me + reach(g) < length)
+
+    def sends(g):
+        return (me - reach(g) >= 0) & (me - reach(g) < length)
+
     for g in range(GROUPS):
-        pl.semaphore_signal(
-            barrier,
-            inc=1,
-            device_id=(partner(me, g, length),),
-            device_id_type=pl.DeviceIdType.MESH,
-        )
+
+        @pl.when(receives(g))
+        def _():
+            pl.semaphore_signal(
+                barrier,
+                inc=1,
+                device_id=(partner(me, g, length),),
+                device_id_type=pl.DeviceIdType.MESH,
+            )
+
+    def start(copy, g):
+        @pl.when(receives(g))
+        def _():
+            copy.start()
+
+    def wait(copy, g):
+        @pl.when(sends(g))
+        def _():
+            copy.wait_recv()
+
+    def wait_sent(copy, g):
+        @pl.when(receives(g))
+        def _():
+            copy.wait_send()
 
     def partial_copy(step, g):
         return pltpu.make_async_remote_copy(
-            src_ref=leaving.at[pl.ds(SLOTS * g, SLOTS)],
-            dst_ref=table.at[pl.ds(1 + OWN + SLOTS * g, SLOTS)],
+            src_ref=leaving.at[pl.ds(SENT * g, SENT)],
+            dst_ref=table.at[pl.ds(1 + OWN + SLOTS * g, SENT)],
             send_sem=send_sem.at[step, 0, g],
             recv_sem=recv_sem.at[step, 0, g],
             device_id=(partner(me, g, length),),
@@ -179,15 +220,6 @@
             device_id=(partner(me, g, length),),
             device_id_type=pl.DeviceIdType.MESH,
         )
-
-    def drop_outside(ref, g):
-        source = me - (g + 1) if g < HOPS else me + (g - HOPS + 1)
-
-        @pl.when((source < 0) | (source >= length))
-        def _():
-            ref[1 + OWN + SLOTS * g : 1 + OWN + SLOTS * (g + 1)] = jnp.zeros(
-                (SLOTS, 8, 128), jnp.float32
-            )
 
     row_id = lax.broadcasted_iota(jnp.int32, (8, 128), 0)
     lane_id = lax.broadcasted_iota(jnp.int32, (8, 128), 1)
@@ -232,6 +264,14 @@
     plastic[...] = plastic_in[...]
     table[0] = zero_tile
     padded[0] = zero_tile
+    for g in range(GROUPS):
+
+        @pl.when(jnp.logical_not(sends(g)))
+        def _():
+            for k in range(SENT):
+                table[1 + OWN + SLOTS * g + k] = zero_tile
+            for k in range(3):
+                speed_in[3 * g + k] = zero_tile
 
     def one_step(step, carry):
         def particles(r, carry):
@@ -307,12 +347,11 @@
             tile_b = pair(spots_b, b)
             lines = [tile_a[k : k + 1] for k in range(8)] + [tile_b[k : k + 1] for k in range(7)]
             first, second, third = lines[0:5], lines[5:10], lines[10:15]
-            base = consts[80:88, :]
-            base = jnp.concatenate([base, base], axis=1)
             blocks = [[], [], []]
             weights = []
             for a in range(3):
-                node = base + float(a)
+                node = consts[80 + 8 * a : 88 + 8 * a, :]
+                node = jnp.concatenate([node, node], axis=1)
                 w = weight(node, first)
                 d = w * (node - first[1])
                 weights.append((w, d))
@@ -341,28 +380,50 @@
             both = dot_nt(lhs, high) + dot_nt(lhs, low)
             total = both[0:24] + both[24:48]
             block = jnp.concatenate(
-                [total[0:8, 0:36], total[8:16, 0:36], total[16:24, 0:36], zero_tile[:, 0:20]],
+                [
+                    total[0:8, 0:36],
+                    total[8:16, 0:RIM],
+                    total[16:24, 0:RIM],
+                    total[8:16, RIM:36],
+                    total[16:24, RIM:36],
+                    zero_tile[:, 0:20],
+                ],
                 axis=1,
             )
             own[b] = block
             table[1 + b] = block
             return carry
 
-        lax.fori_loop(0, OWN, scatter, 0, unroll=8)
+        lax.fori_loop(0, OWN, scatter, 0, unroll=16)
 
         @pl.when(step == 0)
         def _():
-            pl.semaphore_wait(barrier, GROUPS)
-
-        for g in range(GROUPS):
-            for k in range(SLOTS):
-                leaving[SLOTS * g + k] = own[rows[0, SLOTS * g + k]]
-            partial_copy(step, g).start()
-        for g in range(GROUPS):
-            partial_copy(step, g).wait()
-            drop_outside(table, g)
-
-        offset_id = consts[88:96, :]
+            pl.semaphore_wait(
+                barrier, jnp.minimum(me, HOPS) + jnp.minimum(length - 1 - me, HOPS)
+            )
+
+        for g in FAR_FIRST:
+            tiles = [own[rows[0, SLOTS * g + k]] for k in range(SLOTS)]
+            for m in range(SLOTS - SENT):
+                third = tiles[SENT + m]
+                for k, by in ((2 * m, USED), (2 * m + 1, 2 * USED - 128)):
+                    leaving[SENT * g + k] = jnp.where(
+                        lane_id < USED, tiles[k], pltpu.roll(third, by, 1)
+                    )
+            start(partial_copy(step, g), g)
+        for g in NEAR_FIRST:
+            wait(partial_copy(step, g), g)
+            at = 1 + OWN + SLOTS * g
+            for m in range(SLOTS - SENT):
+                table[at + SENT + m] = jnp.where(
+                    lane_id < 128 - USED,
+                    pltpu.roll(table[at + 2 * m], 128 - USED, 1),
+                    pltpu.roll(table[at + 2 * m + 1], 256 - 2 * USED, 1),
+                )
+        for g in FAR_FIRST:
+            wait_sent(partial_copy(step, g), g)
+
+        offset_id = consts[104:112, :]
 
         def collect(o, total):
             here = offset_id == o.astype(jnp.float32)
@@ -370,7 +431,7 @@
                 jnp.where(here, table[1 + links[b, o]], total[b]) for b in range(OWN)
             )
 
-        total = lax.fori_loop(0, 27, collect, (zero_tile,) * OWN)
+        total = lax.fori_loop(0, 27, collect, (zero_tile,) * OWN, unroll=27)
         total = dot_nn(high_low(jnp.concatenate(total, axis=0), 1), fold_mats[0])
         for b in range(OWN):
             node = total[8 * b : 8 * b + 8]
@@ -385,21 +446,21 @@
             speed[b] = node
             speed_side[b] = pltpu.roll(node, 64, 1)
 
-        for g in range(GROUPS):
+        for g in FAR_FIRST:
             for m in range(3):
                 r = [rows[0, SLOTS * g + 4 * m + k] for k in range(4)]
                 speed_out[3 * g + m] = jnp.where(upper, speed[r[0]], speed[r[1]]) + jnp.where(
                     upper, speed_side[r[2]], speed_side[r[3]]
                 )
-            speed_copy(step, g).start()
+            start(speed_copy(step, g), g)
 
         def spread(tiles):
             x = high_low(jnp.concatenate(tiles, axis=0), 1)
             return dot_nn(x, fold_mats[1]).reshape(len(tiles), 8, 128)
 
         padded[1 : 1 + OWN] = spread([speed[b] for b in range(OWN)])
-        for g in range(GROUPS):
-            speed_copy(step, g).wait()
+        for g in NEAR_FIRST:
+            wait(speed_copy(step, g), g)
             tiles = []
             for m in range(3):
                 z = speed_in[3 * g + m]
@@ -411,7 +472,6 @@
                 tiles.append(jnp.where(upper_left, zl, jnp.where(lower_right, zs, 0.0)))
                 tiles.append(jnp.where(upper_left, zs, jnp.where(lower_right, zl, 0.0)))
             padded[1 + OWN + SLOTS * g : 1 + OWN + SLOTS * (g + 1)] = spread(tiles)
-            drop_outside(padded, g)
 
         def fetch(o, total):
             here = offset_id == (26 - o).astype(jnp.float32)
@@ -419,7 +479,10 @@
                 jnp.where(here, padded[1 + links[b, o]], total[b]) for b in range(OWN)
             )
 
-        total = lax.fori_loop(0, 27, fetch, (zero_tile,) * OWN)
+        for g in FAR_FIRST:
+            wait_sent(speed_copy(step, g), g)
+
+        total = lax.fori_loop(0, 27, fetch, (zero_tile,) * OWN, unroll=27)
         for b in range(OWN):
             field[b] = total[b]
 
@@ -427,7 +490,15 @@
 
         def gather(b, carry):
             v = field[b]
-            v = jnp.concatenate([v[:, 0:48], v[:, 36:84], v[:, 72:120]], axis=0)
+            fill = zero_tile[:, 0:12]
+            v = jnp.concatenate(
+                [
+                    jnp.concatenate([v[:, 0:36], fill], axis=1),
+                    jnp.concatenate([v[:, 36:56], v[:, 76:92], fill], axis=1),
+                    jnp.concatenate([v[:, 56:76], v[:, 92:108], fill], axis=1),
+                ],
+                axis=0,
+            )
             v = high_low(v, 0)
             spot = pl.ds(pl.multiple_of(48 * b, 16), 48)
             both = dot_nn(v, weight_hi[spot, :]) + dot_nn(v, weight_lo[spot, :])
@@ -450,7 +521,7 @@
             found_b[spot, :] = jnp.concatenate([out[:, 0:128], out[:, 128:256]], axis=0)
             return carry
 
-        lax.fori_loop(0, OWN, gather, 0, unroll=8)
+        lax.fori_loop(0, OWN, gather, 0, unroll=16)
 
         def finish(r, carry):
             band = pl.ds(pl.multiple_of(8 * r, 8), 8)
@@ -564,7 +635,7 @@
             pltpu.VMEM(row9, f32),
             pltpu.VMEM(planar, f32),
             pltpu.VMEM(planar, f32),
-            pltpu.VMEM((96, 128), f32),
+            pltpu.VMEM((112, 128), f32),
             pltpu.VMEM((2, 256, 128), jnp.bfloat16),
             tile,
             tile,
@@ -583,7 +654,7 @@
             pltpu.VMEM((24 * OWN, PMAX), f32),
             pltpu.VMEM((OWN, 8, 128), f32),
             pltpu.VMEM((TABLE, 8, 128), f32),
-            pltpu.VMEM((RECEIVED, 8, 128), f32),
+            pltpu.VMEM((SENT * GROUPS, 8, 128), f32),
             pltpu.VMEM((OWN, 8, 128), f32),
             pltpu.VMEM((OWN, 8, 128), f32),
             pltpu.VMEM((3 * GROUPS, 8, 128), f32),

time: 59.9 us -> 51.8 us (0.86)
  the two profiles are of different devices: /device:TPU:1 before, /device:TPU:32 now
where the time goes in v3:
time: 51.8 us; the launch traced here: 51.7 us
  Pallas kernels  51 us (98%)
  between operations  0.64 us (1%)
    pallas_call x1, Pallas kernels, on_device(): pl.pallas_call(lambda *refs: step_kernel(length, *refs), out_shape=shapes...  49.1 us
    pallas_call x1, Pallas kernels, on_device(): pl.pallas_call(hand_over, out_shape=shapes, in_specs=[hbm] * 5, out_specs...  1.91 us

profile of v3, /device:TPU:32, one launch (start us, length us, event | category | flops | bytes accessed | tf_op | source)
XLA Modules:
  0.0 51.7 jit_solution(6855269208214875158)
XLA Ops:
  0.6 49.1 %snow_steps.1 = (f32[3,4096]{1,0:T(4,128)}, f32[3,4096]{1,0:T(4,128)}, f32[9,4096]{1,0:T(8,128)}, f32[9,4096]{1,0:T(8,128)}, f32[32,128]{1,0:T(8,128)}) custom-call(s32[16,27]{1,0:T(8,128)} %refs_0_.1, s32[1,96]{1,0:T(1,128)} %refs_1_.1, s32[16]{0:T(128)} %refs_2_.1, s32[32,128]{1,0:T(8,128)} %bitcast.4, f32[3,4096]{1,0:T(4,128)} %refs_4_.1, ...), custom_call_target="tpu_custom_call" | custom-call | tf_op jit(solution)/shard_map/snow_steps/pallas_call | solution.py:622
  49.8 1.9 %hand_over.1 = (f32[3,4096]{1,0:T(4,128)}, f32[3,4096]{1,0:T(4,128)}, f32[9,4096]{1,0:T(8,128)}, f32[9,4096]{1,0:T(8,128)}, f32[32,128]{1,0:T(8,128)}) custom-call(f32[3,4096]{1,0:T(4,128)} %get-tuple-element.15.refs_0_, f32[3,4096]{1,0:T(4,128)} %get-tuple-element.16.refs_1_, f32[9,4096]{1,0:T(8,128)} %get-tuple-element.17.refs_2_, ...), custom_call_target="tpu_custom_call" | custom-call | tf_op jit(solution)/shard_map/hand_over/pallas_call | solution.py:688

commit v4 on v3

--- a/solution.py
+++ b/solution.py
@@ -18,6 +18,7 @@
 RIM = 20
 USED = 36 + 2 * RIM
 SENT = 8
+RING = 16
 FAR_FIRST = (3, 7, 2, 6, 1, 5, 0, 4)
 NEAR_FIRST = (0, 4, 1, 5, 2, 6, 3, 7)
 
@@ -65,7 +66,7 @@
             np.where(half == 0, 2, 3),
             offset_id,
         ]
-    ).astype(np.float32)
+    ).astype(np.int32)
     folds = np.stack([np.concatenate([fold, fold]), np.concatenate([fold.T, fold.T])])
     return consts, folds
 
@@ -185,6 +186,17 @@
                 device_id=(partner(me, g, length),),
                 device_id_type=pl.DeviceIdType.MESH,
             )
+
+    depth = lax.rem(me, RING)
+
+    def in_turn(send):
+        @pl.when(depth < RING // 2)
+        def _():
+            send((7, 6, 5, 4, 3, 2, 1, 0))
+
+        @pl.when(depth >= RING // 2)
+        def _():
+            send((3, 2, 1, 0, 7, 6, 5, 4))
 
     def start(copy, g):
         @pl.when(receives(g))
@@ -340,6 +352,24 @@
 
         lax.fori_loop(0, TILES // 8, particles, 0)
 
+        places = lax.broadcasted_iota(jnp.int32, (8, PMAX), 0).astype(jnp.float32)
+
+        def spline_rows(spots):
+            w = weight(places, spots)
+            return w, w * (places - spots[1])
+
+        def spread_rows(x, at, count):
+            parts = []
+            for k in range(0, count, 8):
+                index = consts[at + k : at + k + 8, :]
+                parts.append(
+                    jnp.concatenate(
+                        [jnp.take_along_axis(x[:, l : l + 128], index, axis=0) for l in (0, 128)],
+                        axis=1,
+                    )
+                )
+            return jnp.concatenate(parts, axis=0)
+
         def scatter(b, carry):
             mass_flow = pair(part_a, b)
             push = [pair(part_b, b), pair(part_c, b), pair(part_d, b)]
@@ -349,11 +379,9 @@
             first, second, third = lines[0:5], lines[5:10], lines[10:15]
             blocks = [[], [], []]
             weights = []
+            first_pair = spline_rows(first)
             for a in range(3):
-                node = consts[80 + 8 * a : 88 + 8 * a, :]
-                node = jnp.concatenate([node, node], axis=1)
-                w = weight(node, first)
-                d = w * (node - first[1])
+                w, d = (spread_rows(x, 80 + 8 * a, 8) for x in first_pair)
                 weights.append((w, d))
                 blocks[0].append(w * mass_flow + d * push[0])
                 blocks[1].append(w * push[1])
@@ -362,13 +390,10 @@
             first_w[spot, :] = jnp.concatenate([w for w, d in weights], axis=0)
             first_d[spot, :] = jnp.concatenate([d for w, d in weights], axis=0)
             lhs = jnp.concatenate([jnp.concatenate(x, axis=0) for x in blocks], axis=1)
-            node2 = consts[0:40, :]
-            node2 = jnp.concatenate([node2, node2], axis=1)
-            node3 = consts[40:80, :]
-            node3 = jnp.concatenate([node3, node3], axis=1)
-            w23 = weight(node2, second) * weight(node3, third)
+            second_w, second_d = (spread_rows(x, 0, 40) for x in spline_rows(second))
+            third_w, third_d = (spread_rows(x, 40, 40) for x in spline_rows(third))
             rhs = jnp.concatenate(
-                [w23, w23 * (node2 - second[1]), w23 * (node3 - third[1])], axis=1
+                [second_w * third_w, second_d * third_w, second_w * third_d], axis=1
             )
             rhs = jnp.concatenate([rhs, jnp.zeros((8, 3 * PMAX), jnp.float32)], axis=0)
             high = rhs.astype(jnp.bfloat16)
@@ -402,15 +427,18 @@
                 barrier, jnp.minimum(me, HOPS) + jnp.minimum(length - 1 - me, HOPS)
             )
 
-        for g in FAR_FIRST:
-            tiles = [own[rows[0, SLOTS * g + k]] for k in range(SLOTS)]
-            for m in range(SLOTS - SENT):
-                third = tiles[SENT + m]
-                for k, by in ((2 * m, USED), (2 * m + 1, 2 * USED - 128)):
-                    leaving[SENT * g + k] = jnp.where(
-                        lane_id < USED, tiles[k], pltpu.roll(third, by, 1)
-                    )
-            start(partial_copy(step, g), g)
+        def send_partials(order):
+            for g in order:
+                tiles = [own[rows[0, SLOTS * g + k]] for k in range(SLOTS)]
+                for m in range(SLOTS - SENT):
+                    third = tiles[SENT + m]
+                    for k, by in ((2 * m, USED), (2 * m + 1, 2 * USED - 128)):
+                        leaving[SENT * g + k] = jnp.where(
+                            lane_id < USED, tiles[k], pltpu.roll(third, by, 1)
+                        )
+                start(partial_copy(step, g), g)
+
+        in_turn(send_partials)
         for g in NEAR_FIRST:
             wait(partial_copy(step, g), g)
             at = 1 + OWN + SLOTS * g
@@ -426,7 +454,7 @@
         offset_id = consts[104:112, :]
 
         def collect(o, total):
-            here = offset_id == o.astype(jnp.float32)
+            here = offset_id == o
             return tuple(
                 jnp.where(here, table[1 + links[b, o]], total[b]) for b in range(OWN)
             )
@@ -446,35 +474,43 @@
             speed[b] = node
             speed_side[b] = pltpu.roll(node, 64, 1)
 
-        for g in FAR_FIRST:
-            for m in range(3):
-                r = [rows[0, SLOTS * g + 4 * m + k] for k in range(4)]
-                speed_out[3 * g + m] = jnp.where(upper, speed[r[0]], speed[r[1]]) + jnp.where(
-                    upper, speed_side[r[2]], speed_side[r[3]]
-                )
-            start(speed_copy(step, g), g)
+        def send_speeds(order):
+            for g in order:
+                for m in range(3):
+                    r = [rows[0, SLOTS * g + 4 * m + k] for k in range(4)]
+                    speed_out[3 * g + m] = jnp.where(
+                        upper, speed[r[0]], speed[r[1]]
+                    ) + jnp.where(upper, speed_side[r[2]], speed_side[r[3]])
+                start(speed_copy(step, g), g)
+
+        in_turn(send_speeds)
 
         def spread(tiles):
             x = high_low(jnp.concatenate(tiles, axis=0), 1)
             return dot_nn(x, fold_mats[1]).reshape(len(tiles), 8, 128)
 
         padded[1 : 1 + OWN] = spread([speed[b] for b in range(OWN)])
-        for g in NEAR_FIRST:
-            wait(speed_copy(step, g), g)
+        for batch in (NEAR_FIRST[0:4], NEAR_FIRST[4:8]):
+            for g in batch:
+                wait(speed_copy(step, g), g)
             tiles = []
-            for m in range(3):
-                z = speed_in[3 * g + m]
-                zs = pltpu.roll(z, 4, 0)
-                zl = pltpu.roll(z, 64, 1)
-                zd = pltpu.roll(zs, 64, 1)
-                tiles.append(jnp.where(upper_left, z, jnp.where(lower_right, zd, 0.0)))
-                tiles.append(jnp.where(upper_left, zd, jnp.where(lower_right, z, 0.0)))
-                tiles.append(jnp.where(upper_left, zl, jnp.where(lower_right, zs, 0.0)))
-                tiles.append(jnp.where(upper_left, zs, jnp.where(lower_right, zl, 0.0)))
-            padded[1 + OWN + SLOTS * g : 1 + OWN + SLOTS * (g + 1)] = spread(tiles)
+            for g in batch:
+                for m in range(3):
+                    z = speed_in[3 * g + m]
+                    zs = pltpu.roll(z, 4, 0)
+                    zl = pltpu.roll(z, 64, 1)
+                    zd = pltpu.roll(zs, 64, 1)
+                    tiles.append(jnp.where(upper_left, z, jnp.where(lower_right, zd, 0.0)))
+                    tiles.append(jnp.where(upper_left, zd, jnp.where(lower_right, z, 0.0)))
+                    tiles.append(jnp.where(upper_left, zl, jnp.where(lower_right, zs, 0.0)))
+                    tiles.append(jnp.where(upper_left, zs, jnp.where(lower_right, zl, 0.0)))
+            tiles = spread(tiles)
+            for k, g in enumerate(batch):
+                at = 1 + OWN + SLOTS * g
+                padded[at : at + SLOTS] = tiles[SLOTS * k : SLOTS * (k + 1)]
 
         def fetch(o, total):
-            here = offset_id == (26 - o).astype(jnp.float32)
+            here = offset_id == 26 - o
             return tuple(
                 jnp.where(here, padded[1 + links[b, o]], total[b]) for b in range(OWN)
             )
@@ -635,7 +671,7 @@
             pltpu.VMEM(row9, f32),
             pltpu.VMEM(planar, f32),
             pltpu.VMEM(planar, f32),
-            pltpu.VMEM((112, 128), f32),
+            pltpu.VMEM((112, 128), i32),
             pltpu.VMEM((2, 256, 128), jnp.bfloat16),
             tile,
             tile,

time: 51.8 us -> 50 us (0.965)
  Pallas kernels: 51 us -> 49.2 us
    pallas_call x1, Pallas kernels: 49.1 us -> 47.3 us  [on_device(): pl.pallas_call(lambda *refs: step_kernel(length, *refs), out_shape=shapes...]
where the time goes in v4:
time: 50 us; the launch traced here: 49.9 us
  Pallas kernels  49.2 us (98%)
  between operations  0.64 us (1%)
    pallas_call x1, Pallas kernels, on_device(): pl.pallas_call(lambda *refs: step_kernel(length, *refs), out_shape=shapes...  47.3 us
    pallas_call x1, Pallas kernels, on_device(): pl.pallas_call(hand_over, out_shape=shapes, in_specs=[hbm] * 5, out_specs...  1.91 us

profile of v4, /device:TPU:32, one launch (start us, length us, event | category | flops | bytes accessed | tf_op | source)
XLA Modules:
  0.0 49.9 jit_solution(3917560279016729740)
XLA Ops:
  0.6 47.3 %snow_steps.1 = (f32[3,4096]{1,0:T(4,128)}, f32[3,4096]{1,0:T(4,128)}, f32[9,4096]{1,0:T(8,128)}, f32[9,4096]{1,0:T(8,128)}, f32[32,128]{1,0:T(8,128)}) custom-call(s32[16,27]{1,0:T(8,128)} %refs_0_.1, s32[1,96]{1,0:T(1,128)} %refs_1_.1, s32[16]{0:T(128)} %refs_2_.1, s32[32,128]{1,0:T(8,128)} %bitcast.4, f32[3,4096]{1,0:T(4,128)} %refs_4_.1, ...), custom_call_target="tpu_custom_call" | custom-call | tf_op jit(solution)/shard_map/snow_steps/pallas_call | solution.py:658
  48.0 1.9 %hand_over.1 = (f32[3,4096]{1,0:T(4,128)}, f32[3,4096]{1,0:T(4,128)}, f32[9,4096]{1,0:T(8,128)}, f32[9,4096]{1,0:T(8,128)}, f32[32,128]{1,0:T(8,128)}) custom-call(f32[3,4096]{1,0:T(4,128)} %get-tuple-element.15.refs_0_, f32[3,4096]{1,0:T(4,128)} %get-tuple-element.16.refs_1_, f32[9,4096]{1,0:T(8,128)} %get-tuple-element.17.refs_2_, ...), custom_call_target="tpu_custom_call" | custom-call | tf_op jit(solution)/shard_map/hand_over/pallas_call | solution.py:724

commit v5 on v4

--- a/solution.py
+++ b/solution.py
@@ -145,8 +145,7 @@
         part_d,
         spots_a,
         spots_b,
-        weight_hi,
-        weight_lo,
+        products,
         first_w,
         first_d,
         own,
@@ -164,9 +163,6 @@
         recv_sem,
         load_sem,
     ) = work
-    loads = [pltpu.make_async_copy(given[k], held[k], load_sem.at[k]) for k in range(12)]
-    for copy in loads:
-        copy.start()
     me = lax.axis_index("dom")
     barrier = pltpu.get_barrier_semaphore()
 
@@ -186,6 +182,10 @@
                 device_id=(partner(me, g, length),),
                 device_id_type=pl.DeviceIdType.MESH,
             )
+
+    loads = [pltpu.make_async_copy(given[k], held[k], load_sem.at[k]) for k in range(12)]
+    for copy in loads:
+        copy.start()
 
     depth = lax.rem(me, RING)
 
@@ -396,13 +396,10 @@
                 [second_w * third_w, second_d * third_w, second_w * third_d], axis=1
             )
             rhs = jnp.concatenate([rhs, jnp.zeros((8, 3 * PMAX), jnp.float32)], axis=0)
-            high = rhs.astype(jnp.bfloat16)
-            low = low_part(rhs).astype(jnp.bfloat16)
-            spot = pl.ds(pl.multiple_of(48 * b, 16), 48)
-            weight_hi[spot, :] = high
-            weight_lo[spot, :] = low
+            rhs = high_low(rhs, 0)
+            products[pl.ds(pl.multiple_of(96 * b, 16), 96), :] = rhs
             lhs = high_low(lhs, 0)
-            both = dot_nt(lhs, high) + dot_nt(lhs, low)
+            both = dot_nt(lhs, rhs[0:48]) + dot_nt(lhs, rhs[48:96])
             total = both[0:24] + both[24:48]
             block = jnp.concatenate(
                 [
@@ -439,8 +436,15 @@
                 start(partial_copy(step, g), g)
 
         in_turn(send_partials)
+
+        @pl.when(step == 1)
+        def _():
+            for g in FAR_FIRST:
+                wait_sent(speed_copy(0, g), g)
+
         for g in NEAR_FIRST:
             wait(partial_copy(step, g), g)
+        for g in range(GROUPS):
             at = 1 + OWN + SLOTS * g
             for m in range(SLOTS - SENT):
                 table[at + SENT + m] = jnp.where(
@@ -448,8 +452,6 @@
                     pltpu.roll(table[at + 2 * m], 128 - USED, 1),
                     pltpu.roll(table[at + 2 * m + 1], 256 - 2 * USED, 1),
                 )
-        for g in FAR_FIRST:
-            wait_sent(partial_copy(step, g), g)
 
         offset_id = consts[104:112, :]
 
@@ -484,6 +486,8 @@
                 start(speed_copy(step, g), g)
 
         in_turn(send_speeds)
+        for g in FAR_FIRST:
+            wait_sent(partial_copy(step, g), g)
 
         def spread(tiles):
             x = high_low(jnp.concatenate(tiles, axis=0), 1)
@@ -515,9 +519,6 @@
                 jnp.where(here, padded[1 + links[b, o]], total[b]) for b in range(OWN)
             )
 
-        for g in FAR_FIRST:
-            wait_sent(speed_copy(step, g), g)
-
         total = lax.fori_loop(0, 27, fetch, (zero_tile,) * OWN, unroll=27)
         for b in range(OWN):
             field[b] = total[b]
@@ -535,9 +536,8 @@
                 ],
                 axis=0,
             )
-            v = high_low(v, 0)
-            spot = pl.ds(pl.multiple_of(48 * b, 16), 48)
-            both = dot_nn(v, weight_hi[spot, :]) + dot_nn(v, weight_lo[spot, :])
+            v = high_low(jnp.concatenate([v, v], axis=1), 0)
+            both = dot_nn(v, products[pl.ds(pl.multiple_of(96 * b, 16), 96), :])
             result = both[0:24] + both[24:48]
             spot = pl.ds(pl.multiple_of(24 * b, 8), 24)
 
@@ -600,6 +600,8 @@
         return carry
 
     lax.fori_loop(0, 2, one_step, 0)
+    for g in FAR_FIRST:
+        wait_sent(speed_copy(1, g), g)
 
     def store_tile(t, carry):
         lanes = pl.ds(pl.multiple_of(128 * t, 128), 128)
@@ -684,8 +686,7 @@
             tile,
             tile,
             tile,
-            pltpu.VMEM((48 * OWN, 3 * PMAX), jnp.bfloat16),
-            pltpu.VMEM((48 * OWN, 3 * PMAX), jnp.bfloat16),
+            pltpu.VMEM((96 * OWN, 3 * PMAX), jnp.bfloat16),
             pltpu.VMEM((24 * OWN, PMAX), f32),
             pltpu.VMEM((24 * OWN, PMAX), f32),
             pltpu.VMEM((OWN, 8, 128), f32),

time: 50 us -> 49.5 us (0.990)
  Pallas kernels: 49.2 us -> 48.7 us
    pallas_call x1, Pallas kernels: 47.3 us -> 46.8 us  [on_device(): pl.pallas_call(lambda *refs: step_kernel(length, *refs), out_shape=shapes...]
where the time goes in v5:
time: 49.5 us; the launch traced here: 49.3 us
  Pallas kernels  48.7 us (98%)
  between operations  0.64 us (1%)
    pallas_call x1, Pallas kernels, on_device(): pl.pallas_call(lambda *refs: step_kernel(length, *refs), out_shape=shapes...  46.8 us
    pallas_call x1, Pallas kernels, on_device(): pl.pallas_call(hand_over, out_shape=shapes, in_specs=[hbm] * 5, out_specs...  1.91 us

profile of v5, /device:TPU:32, one launch (start us, length us, event | category | flops | bytes accessed | tf_op | source)
XLA Modules:
  0.0 49.3 jit_solution(13307449541055443237)
XLA Ops:
  0.6 46.8 %snow_steps.1 = (f32[3,4096]{1,0:T(4,128)}, f32[3,4096]{1,0:T(4,128)}, f32[9,4096]{1,0:T(8,128)}, f32[9,4096]{1,0:T(8,128)}, f32[32,128]{1,0:T(8,128)}) custom-call(s32[16,27]{1,0:T(8,128)} %refs_0_.1, s32[1,96]{1,0:T(1,128)} %refs_1_.1, s32[16]{0:T(128)} %refs_2_.1, s32[32,128]{1,0:T(8,128)} %bitcast.4, f32[3,4096]{1,0:T(4,128)} %refs_4_.1, ...), custom_call_target="tpu_custom_call" | custom-call | tf_op jit(solution)/shard_map/snow_steps/pallas_call | solution.py:660
  47.4 1.9 %hand_over.1 = (f32[3,4096]{1,0:T(4,128)}, f32[3,4096]{1,0:T(4,128)}, f32[9,4096]{1,0:T(8,128)}, f32[9,4096]{1,0:T(8,128)}, f32[32,128]{1,0:T(8,128)}) custom-call(f32[3,4096]{1,0:T(4,128)} %get-tuple-element.15.refs_0_, f32[3,4096]{1,0:T(4,128)} %get-tuple-element.16.refs_1_, f32[9,4096]{1,0:T(8,128)} %get-tuple-element.17.refs_2_, ...), custom_call_target="tpu_custom_call" | custom-call | tf_op jit(solution)/shard_map/hand_over/pallas_call | solution.py:725

commit v6 on v5

--- a/solution.py
+++ b/solution.py
@@ -19,6 +19,7 @@
 USED = 36 + 2 * RIM
 SENT = 8
 RING = 16
+OTHERS = tuple(o for o in range(27) if o != 13)
 FAR_FIRST = (3, 7, 2, 6, 1, 5, 0, 4)
 NEAR_FIRST = (0, 4, 1, 5, 2, 6, 3, 7)
 
@@ -184,8 +185,8 @@
             )
 
     loads = [pltpu.make_async_copy(given[k], held[k], load_sem.at[k]) for k in range(12)]
-    for copy in loads:
-        copy.start()
+    for k in (7, 6, 4, 5, 3, 8, 9, 10, 2, 1, 0, 11):
+        loads[k].start()
 
     depth = lax.rem(me, RING)
 
@@ -270,9 +271,11 @@
         spots_b[spot, :] = zero_tile
         return carry
 
-    for copy in loads:
-        copy.wait()
+    for k in (7, 6, 4, 5):
+        loads[k].wait()
     lax.fori_loop(0, TILES, load_tile, 0, unroll=4)
+    for k in (3, 8, 9, 10, 2):
+        loads[k].wait()
     plastic[...] = plastic_in[...]
     table[0] = zero_tile
     padded[0] = zero_tile
@@ -420,6 +423,8 @@
 
         @pl.when(step == 0)
         def _():
+            for k in (1, 0, 11):
+                loads[k].wait()
             pl.semaphore_wait(
                 barrier, jnp.minimum(me, HOPS) + jnp.minimum(length - 1 - me, HOPS)
             )
@@ -461,7 +466,9 @@
                 jnp.where(here, table[1 + links[b, o]], total[b]) for b in range(OWN)
             )
 
-        total = lax.fori_loop(0, 27, collect, (zero_tile,) * OWN, unroll=27)
+        total = tuple(own[b] for b in range(OWN))
+        for o in OTHERS:
+            total = collect(o, total)
         total = dot_nn(high_low(jnp.concatenate(total, axis=0), 1), fold_mats[0])
         for b in range(OWN):
             node = total[8 * b : 8 * b + 8]
@@ -519,7 +526,9 @@
                 jnp.where(here, padded[1 + links[b, o]], total[b]) for b in range(OWN)
             )
 
-        total = lax.fori_loop(0, 27, fetch, (zero_tile,) * OWN, unroll=27)
+        total = tuple(padded[1 + b] for b in range(OWN))
+        for o in OTHERS:
+            total = fetch(o, total)
         for b in range(OWN):
             field[b] = total[b]
 

time: 49.5 us -> 49.5 us (level)
  no operation moved by 1% of the time
where the time goes in v6:
time: 49.5 us; the launch traced here: 49.3 us
  Pallas kernels  48.7 us (98%)
  between operations  0.64 us (1%)
    pallas_call x1, Pallas kernels, on_device(): pl.pallas_call(lambda *refs: step_kernel(length, *refs), out_shape=shapes...  46.8 us
    pallas_call x1, Pallas kernels, on_device(): pl.pallas_call(hand_over, out_shape=shapes, in_specs=[hbm] * 5, out_specs...  1.91 us

profile of v6, /device:TPU:32, one launch (start us, length us, event | category | flops | bytes accessed | tf_op | source)
XLA Modules:
  0.0 49.3 jit_solution(15871745581509113531)
XLA Ops:
  0.6 46.8 %snow_steps.1 = (f32[3,4096]{1,0:T(4,128)}, f32[3,4096]{1,0:T(4,128)}, f32[9,4096]{1,0:T(8,128)}, f32[9,4096]{1,0:T(8,128)}, f32[32,128]{1,0:T(8,128)}) custom-call(s32[16,27]{1,0:T(8,128)} %refs_0_.1, s32[1,96]{1,0:T(1,128)} %refs_1_.1, s32[16]{0:T(128)} %refs_2_.1, s32[32,128]{1,0:T(8,128)} %bitcast.4, f32[3,4096]{1,0:T(4,128)} %refs_4_.1, ...), custom_call_target="tpu_custom_call" | custom-call | tf_op jit(solution)/shard_map/snow_steps/pallas_call | solution.py:669
  47.4 1.9 %hand_over.1 = (f32[3,4096]{1,0:T(4,128)}, f32[3,4096]{1,0:T(4,128)}, f32[9,4096]{1,0:T(8,128)}, f32[9,4096]{1,0:T(8,128)}, f32[32,128]{1,0:T(8,128)}) custom-call(f32[3,4096]{1,0:T(4,128)} %get-tuple-element.15.refs_0_, f32[3,4096]{1,0:T(4,128)} %get-tuple-element.16.refs_1_, f32[9,4096]{1,0:T(8,128)} %get-tuple-element.17.refs_2_, ...), custom_call_target="tpu_custom_call" | custom-call | tf_op jit(solution)/shard_map/hand_over/pallas_call | solution.py:734

commit v7 on v6

--- a/solution.py
+++ b/solution.py
@@ -501,7 +501,7 @@
             return dot_nn(x, fold_mats[1]).reshape(len(tiles), 8, 128)
 
         padded[1 : 1 + OWN] = spread([speed[b] for b in range(OWN)])
-        for batch in (NEAR_FIRST[0:4], NEAR_FIRST[4:8]):
+        for batch in (NEAR_FIRST[0:6], NEAR_FIRST[6:8]):
             for g in batch:
                 wait(speed_copy(step, g), g)
             tiles = []

time: 49.5 us -> 49.8 us (level)
  no operation moved by 1% of the time
where the time goes in v7:
time: 49.8 us; the launch traced here: 49.7 us
  Pallas kernels  49 us (98%)
  between operations  0.64 us (1%)
    pallas_call x1, Pallas kernels, on_device(): pl.pallas_call(lambda *refs: step_kernel(length, *refs), out_shape=shapes...  47.1 us
    pallas_call x1, Pallas kernels, on_device(): pl.pallas_call(hand_over, out_shape=shapes, in_specs=[hbm] * 5, out_specs...  1.91 us

profile of v7, /device:TPU:32, one launch (start us, length us, event | category | flops | bytes accessed | tf_op | source)
XLA Modules:
  0.0 49.7 jit_solution(10719181513371982590)
XLA Ops:
  0.6 47.1 %snow_steps.1 = (f32[3,4096]{1,0:T(4,128)}, f32[3,4096]{1,0:T(4,128)}, f32[9,4096]{1,0:T(8,128)}, f32[9,4096]{1,0:T(8,128)}, f32[32,128]{1,0:T(8,128)}) custom-call(s32[16,27]{1,0:T(8,128)} %refs_0_.1, s32[1,96]{1,0:T(1,128)} %refs_1_.1, s32[16]{0:T(128)} %refs_2_.1, s32[32,128]{1,0:T(8,128)} %bitcast.4, f32[3,4096]{1,0:T(4,128)} %refs_4_.1, ...), custom_call_target="tpu_custom_call" | custom-call | tf_op jit(solution)/shard_map/snow_steps/pallas_call | solution.py:669
  47.8 1.9 %hand_over.1 = (f32[3,4096]{1,0:T(4,128)}, f32[3,4096]{1,0:T(4,128)}, f32[9,4096]{1,0:T(8,128)}, f32[9,4096]{1,0:T(8,128)}, f32[32,128]{1,0:T(8,128)}) custom-call(f32[3,4096]{1,0:T(4,128)} %get-tuple-element.15.refs_0_, f32[3,4096]{1,0:T(4,128)} %get-tuple-element.16.refs_1_, f32[9,4096]{1,0:T(8,128)} %get-tuple-element.17.refs_2_, ...), custom_call_target="tpu_custom_call" | custom-call | tf_op jit(solution)/shard_map/hand_over/pallas_call | solution.py:734
